TPU v7x, 256 devices: a whole 4x4x8 slice. The times are simulated.
256 devices in a mesh: ctx: 64 (over x, z, core), ch: 4 (over y).
Axes of the slice: x: 4, y: 4, z: 8, core: 2. Of those that a mesh axis runs over, the one named last changes fastest.
Arguments:
- query_mr: bfloat16 [8192, 8192], P('ch', 'ctx'), may hold values from -18 to 18
- key_mr: bfloat16 [8192, 8192], P('ch', 'ctx'), may hold values from -6 to 6
- value_mr: bfloat16 [8192, 8192], P('ch', 'ctx'), may hold values from -6 to 6
- key_li: bfloat16 [8192, 8192], P('ch', 'ctx'), may hold values from -6 to 6
- cotangent: bfloat16 [8192, 8192], P('ch', 'ctx'), may hold values from -6 to 6
- norm_gain: float32 [8192], P('ch'), may hold values from 0.5 to 1.5
- filter_mr: float32 [8192, 128], P('ch'), may hold values from -0.5 to 0.5
- filter_li: float32 [8192, 8192], P('ch', 'ctx'), may hold values from -1 to 1
Outputs:
- grad_query: bfloat16 [8192, 8192], P('ch', 'ctx')
- grad_key: bfloat16 [8192, 8192], P('ch', 'ctx')
- grad_value: bfloat16 [8192, 8192], P('ch', 'ctx')
- grad_key_li: bfloat16 [8192, 8192], P('ch', 'ctx')
- grad_gain: float32 [8192], P('ch')
- grad_filter_mr: float32 [8192, 128], P('ch')
- grad_filter_li: float32 [8192, 8192], P('ch', 'ctx')
All inputs are finite; a program needn't handle non-finite values.
Results may differ from a plain program's by a relative error of at most 0.0085.
Values may be sent and summed in bfloat16 or wider, within the bound.
No kernel may reach another device: no remote copies, remote signals or barrier semaphores. Data moves between devices by JAX's collectives and lax.ppermute only.
A program may use at most 128 MiB of HBM per device.

v0:
```python
import functools
import math

import jax
import jax.numpy as jnp
import numpy as np
from jax import lax
from jax.experimental import pallas as pl
from jax.experimental.pallas import tpu as pltpu
from jax.sharding import PartitionSpec as P

D = 8192
LANES = 128
EPSILON = 1e-06
BF16 = jnp.bfloat16
F32 = jnp.float32


def halves(table):
    high = table.astype(np.float32).astype(BF16)
    low = (table - high.astype(np.float64)).astype(np.float32).astype(BF16)
    return jnp.asarray(high), jnp.asarray(low)


def short_tables():
    place = np.arange(2 * LANES)
    angle = 2.0 * math.pi / (2 * LANES) * place[:, None] * (np.arange(LANES)[None, :] + 0.5)
    ahead = np.concatenate([np.cos(angle), -np.sin(angle)], axis=1)
    return halves(ahead) + halves(ahead.T / LANES)


def long_tables(blocks):
    radix = 2 * blocks
    total = radix * LANES
    half = np.arange(blocks) + 0.5
    outer = 2.0 * math.pi / radix * half[:, None] * np.arange(blocks)[None, :]
    first = np.concatenate([np.cos(outer), -np.sin(outer)], axis=0)
    twist = 2.0 * math.pi / total * half[:, None] * np.arange(LANES)[None, :]
    inner = 2.0 * math.pi / LANES * (np.arange(LANES)[:, None] * np.arange(LANES)[None, :] % LANES)
    cosine, sine = np.cos(inner), np.sin(inner)
    second = np.block([[cosine, -sine], [sine, cosine]])
    first_high, first_low = halves(first)
    last_high, last_low = halves(first.T * (2.0 / total))
    return (
        jnp.concatenate([first_high, first_low], axis=1),
        jnp.asarray(np.cos(twist), F32),
        jnp.asarray(np.sin(twist), F32),
        jnp.asarray(second, BF16),
        jnp.asarray(second.T, BF16),
        jnp.concatenate([last_high, last_low], axis=1),
    )


def dot(left, right):
    return jnp.dot(left, right, preferred_element_type=F32)


def split(values):
    high = values.astype(BF16)
    return high, (values - high.astype(F32)).astype(BF16)


def dot3(values, high, low):
    values_high, values_low = split(values)
    return dot(
        jnp.concatenate([values_high, values_low, values_high], axis=1),
        jnp.concatenate([high, high, low], axis=0),
    )


def dot1(values, table):
    return dot(values.astype(BF16), table)


def dot2(values, high, low):
    once = values.astype(BF16)
    return dot(jnp.concatenate([once, once], axis=1), jnp.concatenate([high, low], axis=0))


def product_kernel(key, value, product):
    product[...] = (key[...].astype(F32) * value[...].astype(F32)).astype(BF16)


def pair_kernel(cotan, filt, unread, pair):
    blocks, both = pair.shape[:2]
    pair[:, : both // 2, :] = cotan[...].reshape(blocks, -1, LANES)
    pair[:, both // 2 :, :] = filt[...].astype(BF16).reshape(blocks, -1, LANES)


def gain_column(gain):
    here = lax.broadcasted_iota(jnp.int32, (LANES, LANES), 0)
    diagonal = here == lax.broadcasted_iota(jnp.int32, (LANES, LANES), 1)
    columns = [
        jnp.sum(jnp.where(diagonal, gain[at : at + 1, :], 0.0), axis=1, keepdims=True)
        for at in range(gain.shape[0])
    ]
    return jnp.concatenate(columns, axis=0)


def mr_forward_kernel(
    key, value, prior, query, taps, unread, ahead_high, ahead_low, back_high, back_low,
    conv_out, mixed_out, window_spec, taps_spec, squares,
):
    product = key[...].astype(F32) * value[...].astype(F32)
    window = jnp.concatenate([prior[...].astype(F32), product], axis=1)
    spec = dot3(window, ahead_high[...], ahead_low[...])
    filt = dot3(taps[...], ahead_high[:LANES], ahead_low[:LANES])
    spec_re, spec_im = spec[:, :LANES], spec[:, LANES:]
    filt_re, filt_im = filt[:, :LANES], filt[:, LANES:]
    passed = jnp.concatenate(
        [spec_re * filt_re - spec_im * filt_im, spec_re * filt_im + spec_im * filt_re], axis=1
    )
    conv = dot3(passed, back_high[:, LANES:], back_low[:, LANES:])
    mixed_bf = (query[...].astype(F32) * conv).astype(BF16)
    mixed = mixed_bf.astype(F32)
    conv_out[...] = conv
    mixed_out[...] = mixed_bf
    window_spec[...] = spec
    taps_spec[...] = filt

    @pl.when(pl.program_id(0) == 0)
    def _():
        squares[...] = jnp.zeros_like(squares)

    squares[...] += jnp.sum(mixed * mixed, axis=0, keepdims=True)


def gain_block(gain, count):
    groups = count // LANES
    return gain_column(gain[pl.ds(pl.program_id(0) * groups, groups), :])


def total(parts):
    return functools.reduce(lambda left, right: left + right, [part[...] for part in parts])


def inverse_rms(squares):
    return lax.rsqrt(total(squares) / D + EPSILON)


def mr_project_kernel(grad_signal, key_li, mixed, gain, *rest):
    squares, grad_key_li, project = rest[:-2], rest[-2], rest[-1]
    grad = grad_signal[...].astype(F32)
    scaled = mixed[...].astype(F32) * inverse_rms(squares) * gain_block(gain, mixed.shape[0])
    grad_scaled = grad * scaled
    grad_key_li[...] = grad_scaled.astype(BF16)

    @pl.when(pl.program_id(0) == 0)
    def _():
        project[...] = jnp.zeros_like(project)

    project[...] += jnp.sum(grad_scaled * key_li[...].astype(F32), axis=0, keepdims=True)


def mr_backward_kernel(
    grad_signal, key_li, mixed, conv, query, gain, window_spec, taps_spec,
    ahead_high, ahead_low, back_high, back_low, *rest,
):
    count = (len(rest) - 4) // 2
    project = total(rest[:count]) / D
    grad_query, taps_and_signal, before_grad, own_grad = rest[-4:]
    inv = inverse_rms(rest[count : 2 * count])
    normed = mixed[...].astype(F32) * inv
    gain_col = gain_block(gain, mixed.shape[0])
    gate = key_li[...].astype(F32)
    signal = (normed * gain_col * gate).astype(BF16)
    grad_mixed = inv * (grad_signal[...].astype(F32) * (gate * gain_col) - normed * project)
    grad_query[...] = (grad_mixed * conv[...]).astype(BF16)
    grad_conv = grad_mixed * query[...].astype(F32)
    spec = dot2(grad_conv, ahead_high[LANES:], ahead_low[LANES:])
    spec_re, spec_im = spec[:, :LANES], spec[:, LANES:]

    def against(other):
        other_re, other_im = other[:, :LANES], other[:, LANES:]
        return jnp.concatenate(
            [spec_re * other_re + spec_im * other_im, spec_im * other_re - spec_re * other_im],
            axis=1,
        )

    taps_grad = dot1(against(window_spec[...]), back_high[:, :LANES]).astype(BF16)
    blocks, both_widths = taps_and_signal.shape[:2]
    width = both_widths // 2
    taps_and_signal[:, :width, :] = taps_grad.reshape(blocks, width, LANES)
    taps_and_signal[:, width:, :] = signal.reshape(blocks, width, LANES)
    both = dot1(against(taps_spec[...]), back_high[...])
    before_grad[...] = both[:, :LANES].astype(BF16)
    own_grad[...] = both[:, LANES:]


UNREAD = pl.BlockSpec(memory_space=pltpu.HBM)
LIMIT = pltpu.CompilerParams(vmem_limit_bytes=60 * 1024 * 1024)
PRODUCT_ROWS = 1024
PAIR_ROWS = 1024
FORWARD_ROWS = 1024
PROJECT_ROWS = 1024
BACKWARD_ROWS = 1024


def row_spec(count, width=LANES):
    return pl.BlockSpec((count, width), lambda i: (i, 0))


def whole_spec(shape):
    return pl.BlockSpec(shape, lambda i: (0,) * len(shape))


def by_rows(kernel, name, count, rows, ins, in_specs, outs, out_specs, scratch=()):
    return pl.pallas_call(
        kernel,
        grid=(rows // count,),
        in_specs=in_specs,
        out_specs=out_specs,
        out_shape=[jax.ShapeDtypeStruct(*out) for out in outs],
        scratch_shapes=scratch,
        compiler_params=LIMIT,
        name=name,
    )(*ins)


ROW = ((1, LANES), F32)


def product_of(key, value):
    rows = key.shape[0]
    each = row_spec(PRODUCT_ROWS)
    return by_rows(
        product_kernel, "product_of", PRODUCT_ROWS, rows,
        (key, value), [each] * 2, [((rows, LANES), BF16)], [each],
    )[0]


def pair_up(cotan, filt, after, blocks):
    rows = cotan.shape[0]
    width = rows // blocks
    return by_rows(
        pair_kernel, "pair_up", PAIR_ROWS, rows,
        (cotan, filt, after), [row_spec(PAIR_ROWS)] * 2 + [UNREAD],
        [((blocks, 2 * width, LANES), BF16)],
        [pl.BlockSpec((PAIR_ROWS // width, 2 * width, LANES), lambda i: (i, 0, 0))],
    )[0]


def mr_forward(key, value, prior, query, taps, after, tables):
    rows = key.shape[0]
    each, wide = row_spec(FORWARD_ROWS), row_spec(FORWARD_ROWS, 2 * LANES)
    return by_rows(
        mr_forward_kernel, "mr_forward", FORWARD_ROWS, rows,
        (key, value, prior, query, taps, after, *tables),
        [each] * 5 + [UNREAD] + [whole_spec(table.shape) for table in tables],
        [((rows, LANES), F32), ((rows, LANES), BF16)] + [((rows, 2 * LANES), F32)] * 2 + [ROW],
        [each, each, wide, wide, whole_spec((1, LANES))],
    )


def mr_project(grad_signal, key_li, mixed, gain, squares):
    rows = mixed.shape[0]
    each = row_spec(PROJECT_ROWS)
    return by_rows(
        mr_project_kernel, "mr_project", PROJECT_ROWS, rows,
        (grad_signal, key_li, mixed, gain, *squares),
        [each] * 3 + [whole_spec(gain.shape)] + [whole_spec((1, LANES))] * len(squares),
        [((rows, LANES), BF16), ROW],
        [each, whole_spec((1, LANES))],
    )


def mr_backward(
    grad_signal, key_li, mixed, conv, query, gain, window_spec, taps_spec, tables, project,
    squares, blocks,
):
    rows = mixed.shape[0]
    width = rows // blocks
    each, wide = row_spec(BACKWARD_ROWS), row_spec(BACKWARD_ROWS, 2 * LANES)
    return by_rows(
        mr_backward_kernel, "mr_backward", BACKWARD_ROWS, rows,
        (
            grad_signal, key_li, mixed, conv, query, gain, window_spec, taps_spec,
            *tables, *project, *squares,
        ),
        [each] * 5
        + [whole_spec(gain.shape)]
        + [wide] * 2
        + [whole_spec(table.shape) for table in tables]
        + [whole_spec((1, LANES))] * (len(project) + len(squares)),
        [
            ((rows, LANES), BF16), ((blocks, 2 * width, LANES), BF16), ((rows, LANES), BF16),
            ((rows, LANES), F32),
        ],
        [
            each,
            pl.BlockSpec((BACKWARD_ROWS // width, 2 * width, LANES), lambda i: (i, 0, 0)),
            each,
            each,
        ],
    )


def deliver_kernel(bundled, gain, filter_grad, taps_grad, gain_grad):
    blocks = bundled.shape[0]
    width = filter_grad.shape[0] // blocks
    values = bundled[...].astype(F32)
    filter_grad[...] = values[:, :width, :].reshape(filter_grad.shape)
    taps_grad[...] = values[:, width : 2 * width, :].reshape(taps_grad.shape)
    together = LANES // width
    step = pl.program_id(0)
    row = lax.broadcasted_iota(jnp.int32, (gain.shape[0], blocks), 0)
    block = step * blocks + lax.broadcasted_iota(jnp.int32, (gain.shape[0], blocks), 1)
    own = jnp.where((block >= row * together) & (block < (row + 1) * together), 1.0, 0.0)
    own = own.astype(BF16)
    high = values[:, 2 * width, :].astype(BF16)
    low = values[:, 2 * width + 1, :].astype(BF16)

    @pl.when(step == 0)
    def _():
        gain_grad[...] = jnp.zeros_like(gain_grad)

    gain_grad[...] += dot(own, high) + dot(own, low)

    @pl.when(step == pl.num_programs(0) - 1)
    def _():
        gain_grad[...] = gain_grad[...] / gain[...]


def deliver(bundled, gain, blocks, width):
    each = min(16, blocks)
    rows = row_spec(each * width)
    return by_rows(
        deliver_kernel, "deliver", each, blocks,
        (bundled, gain),
        [
            pl.BlockSpec((each,) + bundled.shape[1:], lambda i: (i, 0, 0)),
            whole_spec(gain.shape),
        ],
        [((blocks * width, LANES), F32)] * 2 + [(gain.shape, F32)],
        [rows, rows, whole_spec(gain.shape)],
    )


EXTRA = 8
GROUP = 8


def channel_rows(channel, blocks, width):
    return pl.ds(channel, blocks, stride=width)


def to_spectrum(flat, channels, blocks, width, offset, first, cosine, sine, second):
    pieces = [flat[channel_rows(offset + c, blocks, width), :].astype(BF16) for c in channels]
    grid = jnp.concatenate(pieces, axis=1)
    outer = dot(first[...], jnp.concatenate([grid, grid], axis=0))
    cos, sin = cosine[...], sine[...]
    turned = []
    for at in range(len(channels)):
        lanes = slice(at * LANES, (at + 1) * LANES)
        real, imag = outer[:blocks, lanes], outer[blocks:, lanes]
        turned.append(
            jnp.concatenate([real * cos + imag * sin, imag * cos - real * sin], axis=1)
        )
    return dot1(jnp.concatenate(turned, axis=0), second[...])


def from_spectrum(spec, count, blocks, second, cosine, sine, last):
    inner = dot1(spec, second[...])
    cos, sin = cosine[...], sine[...]
    turned = []
    for at in range(count):
        rows = slice(at * blocks, (at + 1) * blocks)
        real, imag = inner[rows, :LANES], inner[rows, LANES:]
        turned.append(
            jnp.concatenate([real * cos - imag * sin, imag * cos + real * sin], axis=0)
        )
    once = jnp.concatenate(turned, axis=1).astype(BF16)
    return dot(last[...], jnp.concatenate([once, once], axis=0))


def times_conj(left, right):
    left_re, left_im = left[:, :LANES], left[:, LANES:]
    right_re, right_im = right[:, :LANES], right[:, LANES:]
    return jnp.concatenate(
        [left_re * right_re + left_im * right_im, left_im * right_re - left_re * right_im], axis=1
    )


def signal_grad_kernel(
    blocks, width, pair, unread, first, cosine, sine, second, second_back, last,
    grad_out, cotan_spec, pair_flat, grad_flat,
):
    pair_flat[...] = pair[...].astype(F32)

    def one_group(step, carry):
        channels = [step * GROUP + at for at in range(GROUP)]
        rows = pl.ds(pl.multiple_of(step * (GROUP * blocks), GROUP * blocks), GROUP * blocks)

        def spectrum(offset):
            return to_spectrum(
                pair_flat, channels, blocks, 2 * width, offset, first, cosine, sine, second
            )

        moved = spectrum(0)
        cotan_spec[rows, :] = moved
        grads = from_spectrum(
            times_conj(moved, spectrum(width)), GROUP, blocks, second_back, cosine, sine, last
        )
        for at, channel in enumerate(channels):
            lanes = slice(at * LANES, (at + 1) * LANES)
            grad_flat[channel_rows(channel, blocks, width), :] = grads[:, lanes]
        return carry

    lax.fori_loop(0, width // GROUP, one_group, 0)
    grad_out[...] = grad_flat[...].astype(BF16)


def filter_grad_kernel(
    blocks, width, together, moved, cotan_spec, grad_signal, unread, first, cosine, sine, second,
    second_back, last, bundled, moved_flat, grad_flat,
):
    moved_flat[...] = moved[...].reshape(moved_flat.shape).astype(F32)
    taps = jnp.sum(moved[:, :width, :].astype(F32), axis=0).astype(BF16)
    bundled[:, width : 2 * width, :] = jnp.broadcast_to(taps[None], (blocks, width, LANES))
    terms = moved[:, width:, :].astype(F32) * grad_signal[...].astype(F32)
    sums = jnp.sum(jnp.sum(terms, axis=0), axis=1, keepdims=True)
    high = sums.astype(BF16).astype(F32)
    place = lax.broadcasted_iota(jnp.int32, (width, LANES), 0)
    place = place + lax.rem(lax.axis_index("ctx"), together) * width
    here = lax.broadcasted_iota(jnp.int32, (width, LANES), 1) == place
    lines = [jnp.sum(jnp.where(here, part, 0.0), axis=0) for part in (high, sums - high)]
    row = lax.broadcasted_iota(jnp.int32, (EXTRA, LANES), 0)
    lines = jnp.where(row == 0, lines[0][None], jnp.where(row == 1, lines[1][None], 0.0))
    bundled[:, 2 * width :, :] = jnp.broadcast_to(
        lines.astype(BF16)[None], (blocks, EXTRA, LANES)
    )

    def one_group(step, carry):
        channels = [step * GROUP + at for at in range(GROUP)]
        spec = to_spectrum(
            moved_flat, channels, blocks, 2 * width, width, first, cosine, sine, second
        )
        rows = pl.ds(pl.multiple_of(step * (GROUP * blocks), GROUP * blocks), GROUP * blocks)
        grads = from_spectrum(
            times_conj(cotan_spec[rows, :], spec), GROUP, blocks, second_back, cosine, sine, last
        )
        for at, channel in enumerate(channels):
            lanes = slice(at * LANES, (at + 1) * LANES)
            grad_flat[channel_rows(channel, blocks, width), :] = grads[:, lanes]
        return carry

    lax.fori_loop(0, width // GROUP, one_group, 0)
    bundled[:, :width, :] = grad_flat[...].reshape(blocks, width, LANES).astype(BF16)


def signal_grad(pair, after, blocks, tables):
    rows = pair.shape[0] // 2
    return by_rows(
        functools.partial(signal_grad_kernel, blocks, rows // blocks), "signal_grad", 1, 1,
        (pair, after, *tables),
        [whole_spec(pair.shape), UNREAD] + [whole_spec(table.shape) for table in tables],
        [((rows, LANES), BF16), ((rows, 2 * LANES), F32)],
        [whole_spec((rows, LANES)), whole_spec((rows, 2 * LANES))],
        [pltpu.VMEM((2 * rows, LANES), F32), pltpu.VMEM((rows, LANES), F32)],
    )


def filter_grad(moved, cotan_spec, grad_signal, after, tables):
    blocks, both, _ = moved.shape
    width = both // 2
    ins = (moved, cotan_spec, grad_signal.reshape(blocks, width, LANES))
    shape = (blocks, 2 * width + EXTRA, LANES)
    return by_rows(
        functools.partial(filter_grad_kernel, blocks, width, LANES // width), "filter_grad", 1, 1,
        (*ins, after, *tables),
        [whole_spec(value.shape) for value in ins]
        + [UNREAD]
        + [whole_spec(table.shape) for table in tables],
        [(shape, BF16)],
        [whole_spec(shape)],
        [pltpu.VMEM((2 * blocks * width, LANES), F32), pltpu.VMEM((blocks * width, LANES), F32)],
    )[0]


def swapped(rows):
    return lax.all_to_all(rows, "ctx", split_axis=0, concat_axis=0, tiled=True)


def parts_over_ch(row):
    count = lax.axis_size("ch")
    routes = [[(i, (i + step) % count) for i in range(count)] for step in range(1, count)]
    return [row] + [lax.ppermute(row, "ch", route) for route in routes]


def shifted(block, distance):
    devices = range(lax.axis_size("ctx"))
    route = [(i - distance, i) for i in devices if i - distance in devices]
    return lax.ppermute(block, "ctx", route)


def local(query_mr, key_mr, value_mr, key_li, cotangent, norm_gain, filter_mr, filter_li):
    blocks = lax.axis_size("ctx")
    rows = query_mr.shape[0]
    short = short_tables()
    long = long_tables(blocks)
    width = rows // blocks
    gain = norm_gain.reshape(-1, LANES)
    product = product_of(key_mr, value_mr)
    prior = shifted(product, 1)
    pair = pair_up(cotangent, filter_li, product, blocks)
    moved_pair = swapped(pair).reshape(2 * rows, LANES)
    grad_moved, cotan_spec = signal_grad(moved_pair, prior, blocks, long)
    grad_signal = swapped(grad_moved)
    conv, mixed, window_spec, taps_spec, squares = mr_forward(
        key_mr, value_mr, prior, query_mr, filter_mr, grad_moved, short
    )
    squares = parts_over_ch(squares)
    grad_key_li, terms = mr_project(grad_signal, key_li, mixed, gain, squares)
    grad_query, taps_and_signal, before_grad, own_grad = mr_backward(
        grad_signal, key_li, mixed, conv, query_mr, gain, window_spec, taps_spec, short,
        parts_over_ch(terms), squares, blocks,
    )
    after = shifted(before_grad, -1)
    grad_product = own_grad + after.astype(F32)
    grad_key = (grad_product * value_mr.astype(F32)).astype(BF16)
    grad_value = (grad_product * key_mr.astype(F32)).astype(BF16)
    bundled = filter_grad(swapped(taps_and_signal), cotan_spec, grad_moved, after, long)
    grad_filter_li, grad_filter_mr, gain_rows = deliver(swapped(bundled), gain, blocks, width)
    grad_gain = gain_rows.reshape(rows)
    return (
        grad_query,
        grad_key,
        grad_value,
        grad_key_li,
        grad_gain,
        grad_filter_mr,
        grad_filter_li,
    )


def solution(mesh):
    in_specs = (
        P("ch", "ctx"),
        P("ch", "ctx"),
        P("ch", "ctx"),
        P("ch", "ctx"),
        P("ch", "ctx"),
        P("ch"),
        P("ch", None),
        P("ch", "ctx"),
    )
    out_specs = (
        P("ch", "ctx"),
        P("ch", "ctx"),
        P("ch", "ctx"),
        P("ch", "ctx"),
        P("ch"),
        P("ch", None),
        P("ch", "ctx"),
    )
    return jax.shard_map(local, mesh=mesh, in_specs=in_specs, out_specs=out_specs, check_vma=False)
```

profile of v0, /device:TPU:1, one launch (start us, length us, event | category | flops | bytes accessed | tf_op | source)
XLA Modules:
  0.0 192.0 jit_solution(3530658556131736301)
XLA Ops:
  0.6 2.0 %product_of.1.unread = bf16[2048,128]{1,0:T(8,128)(2,1)} custom-call(bf16[2048,128]{1,0:T(8,128)(2,1)} %key.3, bf16[2048,128]{1,0:T(8,128)(2,1)} %value.3), custom_call_target="tpu_custom_call" | custom-call | tf_op jit(solution)/shard_map/product_of/pallas_call | solution.py:208
  2.6 2.3 %pair_up.1 = bf16[64,64,128]{2,1,0:T(8,128)(2,1)} custom-call(bf16[2048,128]{1,0:T(8,128)(2,1)} %cotan.1, f32[2048,128]{1,0:T(8,128)} %filt.1, bf16[2048,128]{1,0:T(8,128)(2,1)} %product_of.1.unread), custom_call_target="tpu_custom_call" | custom-call | tf_op jit(solution)/shard_map/pair_up/pallas_call | solution.py:208
  4.9 13.0 %all-to-all-start = ((bf16[64,64,128]{2,1,0:T(8,128)(2,1)}), bf16[64,64,128]{2,1,0:T(8,128)(2,1)S(1)}, u32[]{:S(2)}, u32[]{:S(2)}) async-start(bf16[64,64,128]{2,1,0:T(8,128)(2,1)} %pair_up.1), calls=%async_computation | async-start | bytes 2097152 | tf_op jit(solution)/shard_map/all_to_all | solution.py:481
  17.9 3.5 %collective-permute-start = (bf16[2048,128]{1,0:T(8,128)(2,1)S(1)}, bf16[2048,128]{1,0:T(8,128)(2,1)S(1)}, u32[]{:S(2)}, u32[]{:S(2)}) collective-permute-start(bf16[2048,128]{1,0:T(8,128)(2,1)S(1)} %copy-done.6), channel_id=1, source_target_pairs={{0,4},{4,8},{8,12},{12,16},{16,20},{20,24},{24,28},{28,32},{32,36}... | collective-permute-start | bytes 1572872 | tf_op jit(solution)/shard_map/ppermute | solution.py:493
  21.4 24.9 %collective-permute-done.unread.prior = bf16[2048,128]{1,0:T(8,128)(2,1)S(1)} collective-permute-done((bf16[2048,128]{1,0:T(8,128)(2,1)S(1)}, bf16[2048,128]{1,0:T(8,128)(2,1)S(1)}, u32[]{:S(2)}, u32[]{:S(2)}) %collective-permute-start) | collective-permute-done | bytes 524320 | tf_op jit(solution)/shard_map/ppermute | solution.py:493
  46.6 0.5 copy-done.9
  47.1 0.5 copy-done.4
  47.6 6.5 %signal_grad.1 = (bf16[2048,128]{1,0:T(8,128)(2,1)}, f32[2048,256]{1,0:T(8,128)}) custom-call(bf16[4096,128]{1,0:T(8,128)(2,1)} %bitcast.9, bf16[2048,128]{1,0:T(8,128)(2,1)} %copy-done.9, bf16[128,128]{1,0:T(8,128)(2,1)} %constant.36.first, f32[64,128]{1,0:T(8,128)} %constant.32.clone.cosine, f32[64,128]{1,0:T(8,128)} %constant.33.clone.sine, ...), custom_call_target="tpu_custom_call" | custom-call | tf_op jit(solution)/shard_map/signal_grad/pallas_call | solution.py:208
  54.1 11.2 %all-to-all-start.1 = ((bf16[64,32,128]{2,1,0:T(8,128)(2,1)}), bf16[64,32,128]{2,1,0:T(8,128)(2,1)S(1)}, u32[]{:S(2)}, u32[]{:S(2)}) async-start(bf16[64,32,128]{2,1,0:T(8,128)(2,1)} %bitcast.7), calls=%async_computation.1 | async-start | bytes 1048576 | tf_op jit(solution)/shard_map/all_to_all | solution.py:481
  65.4 7.3 %mr_forward.1 = (f32[2048,128]{1,0:T(8,128)}, bf16[2048,128]{1,0:T(8,128)(2,1)}, f32[2048,256]{1,0:T(8,128)}, f32[2048,256]{1,0:T(8,128)}, f32[1,128]{1,0:T(1,128)}) custom-call(bf16[2048,128]{1,0:T(8,128)(2,1)} %key.3, bf16[2048,128]{1,0:T(8,128)(2,1)} %value.3, bf16[2048,128]{1,0:T(8,128)(2,1)} %copy-done.9, bf16[2048,128]{1,0:T(8,128)(2,1)} %query.3, ...), custom_call_target="tpu_custom_call" | custom-call | tf_op jit(solution)/shard_map/mr_forward/pallas_call | solution.py:208
  72.7 2.8 %collective-permute-start.3 = (f32[1,128]{1,0:T(1,128)}, f32[1,128]{1,0:T(1,128)S(1)}, u32[]{:S(2)}, u32[]{:S(2)}) collective-permute-start(f32[1,128]{1,0:T(1,128)} %get-tuple-element.28.rest_0_.rest_4_), channel_id=1, source_target_pairs={{0,3},{1,0},{2,1},{3,2},{4,7},{5,4},{6,5},{7,6},{8,11},{9,8},{10,9... | collective-permute-start | bytes 1544 | tf_op jit(solution)/shard_map/ppermute | solution.py:487
  75.8 0.7 collective-permute-start.1
  76.5 3.3 %collective-permute-done.2.rest_2_.rest_6_ = f32[1,128]{1,0:T(1,128)S(1)} collective-permute-done((f32[1,128]{1,0:T(1,128)}, f32[1,128]{1,0:T(1,128)S(1)}, u32[]{:S(2)}, u32[]{:S(2)}) %collective-permute-start.2) | collective-permute-done | bytes 544 | tf_op jit(solution)/shard_map/ppermute | solution.py:487
  79.8 2.8 %all-to-all-done.1 = bf16[64,32,128]{2,1,0:T(8,128)(2,1)S(1)} async-done(((bf16[64,32,128]{2,1,0:T(8,128)(2,1)}), bf16[64,32,128]{2,1,0:T(8,128)(2,1)S(1)}, u32[]{:S(2)}, u32[]{:S(2)}) %all-to-all-start.1) | async-done | bytes 524320 | tf_op jit(solution)/shard_map/all_to_all | solution.py:481
  82.7 0.8 copy-done
  83.5 2.8 %mr_project.1 = (bf16[2048,128]{1,0:T(8,128)(2,1)}, f32[1,128]{1,0:T(1,128)}) custom-call(bf16[2048,128]{1,0:T(8,128)(2,1)} %bitcast.5, bf16[2048,128]{1,0:T(8,128)(2,1)} %key_li.3, bf16[2048,128]{1,0:T(8,128)(2,1)} %get-tuple-element.24.mixed, f32[16,128]{1,0:T(8,128)} %bitcast.10, f32[1,128]{1,0:T(1,128)} %get-tuple-element.28.rest_0_.rest_4_, ...), custom_call_target="tpu_custom_call" | custom-call | tf_op jit(solution)/shard_map/mr_project/pallas_call | solution.py:208
  86.2 2.7 %collective-permute-start.6 = (f32[1,128]{1,0:T(1,128)}, f32[1,128]{1,0:T(1,128)S(1)}, u32[]{:S(2)}, u32[]{:S(2)}) collective-permute-start(f32[1,128]{1,0:T(1,128)} %get-tuple-element.29.rest_0_), channel_id=1, source_target_pairs={{0,3},{1,0},{2,1},{3,2},{4,7},{5,4},{6,5},{7,6},{8,11},{9,8},{10,9... | collective-permute-start | bytes 1544 | tf_op jit(solution)/shard_map/ppermute | solution.py:487
  89.0 0.3 collective-permute-start.5
  89.3 0.7 collective-permute-start.4
  90.0 2.9 %collective-permute-done.5.rest_2_ = f32[1,128]{1,0:T(1,128)S(1)} collective-permute-done((f32[1,128]{1,0:T(1,128)}, f32[1,128]{1,0:T(1,128)S(1)}, u32[]{:S(2)}, u32[]{:S(2)}) %collective-permute-start.5) | collective-permute-done | bytes 544 | tf_op jit(solution)/shard_map/ppermute | solution.py:487
  93.0 0.5 copy-done.14
  93.6 5.7 %mr_backward.1 = (bf16[2048,128]{1,0:T(8,128)(2,1)}, bf16[64,64,128]{2,1,0:T(8,128)(2,1)}, bf16[2048,128]{1,0:T(8,128)(2,1)}, f32[2048,128]{1,0:T(8,128)}) custom-call(bf16[2048,128]{1,0:T(8,128)(2,1)} %bitcast.6, bf16[2048,128]{1,0:T(8,128)(2,1)} %key_li.3, bf16[2048,128]{1,0:T(8,128)(2,1)} %get-tuple-element.24.mixed, f32[2048,128]{1,0:T(8,128)} %get-tuple-element.25.conv, ...), custom_call_target="tpu_custom_call" | custom-call | tf_op jit(solution)/shard_map/mr_backward/pallas_call | solution.py:208
  99.3 9.1 %all-to-all-start.2 = ((bf16[64,64,128]{2,1,0:T(8,128)(2,1)}), bf16[64,64,128]{2,1,0:T(8,128)(2,1)S(1)}, u32[]{:S(2)}, u32[]{:S(2)}) async-start(bf16[64,64,128]{2,1,0:T(8,128)(2,1)} %get-tuple-element.34), calls=%async_computation.2 | async-start | bytes 2097152 | tf_op jit(solution)/shard_map/all_to_all | solution.py:481
  108.4 2.5 %collective-permute-start.7 = (bf16[2048,128]{1,0:T(8,128)(2,1)S(1)}, bf16[2048,128]{1,0:T(8,128)(2,1)S(1)}, u32[]{:S(2)}, u32[]{:S(2)}) collective-permute-start(bf16[2048,128]{1,0:T(8,128)(2,1)S(1)} %copy-done.16), channel_id=1, source_target_pairs={{4,0},{8,4},{12,8},{16,12},{20,16},{24,20},{28,24},{32,28},{36,32}... | collective-permute-start | bytes 1572872 | tf_op jit(solution)/shard_map/ppermute | solution.py:493
  111.0 27.7 %collective-permute-done.7.unread = bf16[2048,128]{1,0:T(8,128)(2,1)S(1)} collective-permute-done((bf16[2048,128]{1,0:T(8,128)(2,1)S(1)}, bf16[2048,128]{1,0:T(8,128)(2,1)S(1)}, u32[]{:S(2)}, u32[]{:S(2)}) %collective-permute-start.7) | collective-permute-done | bytes 524320 | tf_op jit(solution)/shard_map/ppermute | solution.py:493
  138.7 0.8 copy-done.7
  139.8 6.7 %filter_grad.1 = bf16[64,72,128]{2,1,0:T(8,128)(2,1)} custom-call(bf16[64,64,128]{2,1,0:T(8,128)(2,1)} %copy-done.5, f32[2048,256]{1,0:T(8,128)} %get-tuple-element.35.cotan_spec, bf16[64,32,128]{2,1,0:T(8,128)(2,1)} %bitcast.8, bf16[2048,128]{1,0:T(8,128)(2,1)} %copy-done.7, bf16[128,128]{1,0:T(8,128)(2,1)} %constant.36.first, ...), custom_call_target="tpu_custom_call" | custom-call | tf_op jit(solution)/shard_map/filter_grad/pallas_call | solution.py:208
  146.6 9.1 %all-to-all-start.3 = ((bf16[64,72,128]{2,1,0:T(8,128)(2,1)}), bf16[64,72,128]{2,1,0:T(8,128)(2,1)S(1)}, u32[]{:S(2)}, u32[]{:S(2)}) async-start(bf16[64,72,128]{2,1,0:T(8,128)(2,1)} %filter_grad.1), calls=%async_computation.3 | async-start | bytes 2359296 | tf_op jit(solution)/shard_map/all_to_all | solution.py:481
  155.7 2.5 %multiply_convert_fusion = (bf16[2048,128]{1,0:T(8,128)(2,1)}, bf16[2048,128]{1,0:T(8,128)(2,1)}) fusion(bf16[2048,128]{1,0:T(8,128)(2,1)S(1)} %copy-done.2, f32[2048,128]{1,0:T(8,128)} %get-tuple-element.31, bf16[2048,128]{1,0:T(8,128)(2,1)S(1)} %copy-done.8, bf16[2048,128]{1,0:T(8,128)(2,1)S(1)} %copy-done.3), kind=kLoop, calls=%fused_computation | loop fusion | flops 2097152 | bytes 3670016 | tf_op jit(solution)/shard_map/convert_element_type | solution.py:521
  158.2 28.9 %all-to-all-done.3.bundled = bf16[64,72,128]{2,1,0:T(8,128)(2,1)S(1)} async-done(((bf16[64,72,128]{2,1,0:T(8,128)(2,1)}), bf16[64,72,128]{2,1,0:T(8,128)(2,1)S(1)}, u32[]{:S(2)}, u32[]{:S(2)}) %all-to-all-start.3) | async-done | bytes 1179680 | tf_op jit(solution)/shard_map/all_to_all | solution.py:481
  187.1 1.0 copy-done.1
  188.1 3.9 %deliver.1 = (f32[2048,128]{1,0:T(8,128)}, f32[2048,128]{1,0:T(8,128)}, f32[16,128]{1,0:T(8,128)}) custom-call(bf16[64,72,128]{2,1,0:T(8,128)(2,1)} %copy-done.1, f32[16,128]{1,0:T(8,128)} %bitcast.12), custom_call_target="tpu_custom_call" | custom-call | tf_op jit(solution)/shard_map/deliver/pallas_call | solution.py:208
  (35 shorter events, 1.2 us)
Async XLA Ops:
  2.6 15.3 %copy-start.6 = (bf16[2048,128]{1,0:T(8,128)(2,1)S(1)}, bf16[2048,128]{1,0:T(8,128)(2,1)}, u32[]{:S(2)}) copy-start(bf16[2048,128]{1,0:T(8,128)(2,1)} %product_of.1.unread) | copy-start | bytes 1572868
  4.9 41.7 %all-to-all-start = ((bf16[64,64,128]{2,1,0:T(8,128)(2,1)}), bf16[64,64,128]{2,1,0:T(8,128)(2,1)S(1)}, u32[]{:S(2)}, u32[]{:S(2)}) async-start(bf16[64,64,128]{2,1,0:T(8,128)(2,1)} %pair_up.1), calls=%async_computation | async-start | bytes 2097152 | tf_op jit(solution)/shard_map/all_to_all | solution.py:481
  17.9 28.4 %collective-permute-start = (bf16[2048,128]{1,0:T(8,128)(2,1)S(1)}, bf16[2048,128]{1,0:T(8,128)(2,1)S(1)}, u32[]{:S(2)}, u32[]{:S(2)}) collective-permute-start(bf16[2048,128]{1,0:T(8,128)(2,1)S(1)} %copy-done.6), channel_id=1, source_target_pairs={{0,4},{4,8},{8,12},{12,16},{16,20},{20,24},{24,28},{28,32},{32,36}... | collective-permute-start | bytes 1572872 | tf_op jit(solution)/shard_map/ppermute | solution.py:493
  46.3 0.8 copy-start.9
  46.6 1.0 copy-start.4
  54.1 28.6 %all-to-all-start.1 = ((bf16[64,32,128]{2,1,0:T(8,128)(2,1)}), bf16[64,32,128]{2,1,0:T(8,128)(2,1)S(1)}, u32[]{:S(2)}, u32[]{:S(2)}) async-start(bf16[64,32,128]{2,1,0:T(8,128)(2,1)} %bitcast.7), calls=%async_computation.1 | async-start | bytes 1048576 | tf_op jit(solution)/shard_map/all_to_all | solution.py:481
  72.7 3.9 %collective-permute-start.3 = (f32[1,128]{1,0:T(1,128)}, f32[1,128]{1,0:T(1,128)S(1)}, u32[]{:S(2)}, u32[]{:S(2)}) collective-permute-start(f32[1,128]{1,0:T(1,128)} %get-tuple-element.28.rest_0_.rest_4_), channel_id=1, source_target_pairs={{0,3},{1,0},{2,1},{3,2},{4,7},{5,4},{6,5},{7,6},{8,11},{9,8},{10,9... | collective-permute-start | bytes 1544 | tf_op jit(solution)/shard_map/ppermute | solution.py:487
  75.5 4.3 %collective-permute-start.2 = (f32[1,128]{1,0:T(1,128)}, f32[1,128]{1,0:T(1,128)S(1)}, u32[]{:S(2)}, u32[]{:S(2)}) collective-permute-start(f32[1,128]{1,0:T(1,128)} %get-tuple-element.28.rest_0_.rest_4_), channel_id=1, source_target_pairs={{0,2},{1,3},{2,0},{3,1},{4,6},{5,7},{6,4},{7,5},{8,10},{9,11},{10,... | collective-permute-start | bytes 1544 | tf_op jit(solution)/shard_map/ppermute | solution.py:487
  75.8 4.0 %collective-permute-start.1 = (f32[1,128]{1,0:T(1,128)}, f32[1,128]{1,0:T(1,128)S(1)}, u32[]{:S(2)}, u32[]{:S(2)}) collective-permute-start(f32[1,128]{1,0:T(1,128)} %get-tuple-element.28.rest_0_.rest_4_), channel_id=1, source_target_pairs={{0,1},{1,2},{2,3},{3,0},{4,5},{5,6},{6,7},{7,4},{8,9},{9,10},{10,1... | collective-permute-start | bytes 1544 | tf_op jit(solution)/shard_map/ppermute | solution.py:487
  76.5 6.2 %copy-start.10 = (f32[1,128]{1,0:T(1,128)}, f32[1,128]{1,0:T(1,128)S(1)}, u32[]{:S(2)}) copy-start(f32[1,128]{1,0:T(1,128)S(1)} %collective-permute-done.3.rest_3_.rest_7_) | copy-start | bytes 1540
  79.8 2.9 %copy-start.11 = (f32[1,128]{1,0:T(1,128)}, f32[1,128]{1,0:T(1,128)S(1)}, u32[]{:S(2)}) copy-start(f32[1,128]{1,0:T(1,128)S(1)} %collective-permute-done.2.rest_2_.rest_6_) | copy-start | bytes 1540
  79.8 2.8 %copy-start.12 = (f32[1,128]{1,0:T(1,128)}, f32[1,128]{1,0:T(1,128)S(1)}, u32[]{:S(2)}) copy-start(f32[1,128]{1,0:T(1,128)S(1)} %collective-permute-done.1.rest_1_.rest_5_) | copy-start | bytes 1540
  82.7 0.8 copy-start
  86.2 3.8 %collective-permute-start.6 = (f32[1,128]{1,0:T(1,128)}, f32[1,128]{1,0:T(1,128)S(1)}, u32[]{:S(2)}, u32[]{:S(2)}) collective-permute-start(f32[1,128]{1,0:T(1,128)} %get-tuple-element.29.rest_0_), channel_id=1, source_target_pairs={{0,3},{1,0},{2,1},{3,2},{4,7},{5,4},{6,5},{7,6},{8,11},{9,8},{10,9... | collective-permute-start | bytes 1544 | tf_op jit(solution)/shard_map/ppermute | solution.py:487
  89.0 4.0 %collective-permute-start.5 = (f32[1,128]{1,0:T(1,128)}, f32[1,128]{1,0:T(1,128)S(1)}, u32[]{:S(2)}, u32[]{:S(2)}) collective-permute-start(f32[1,128]{1,0:T(1,128)} %get-tuple-element.29.rest_0_), channel_id=1, source_target_pairs={{0,2},{1,3},{2,0},{3,1},{4,6},{5,7},{6,4},{7,5},{8,10},{9,11},{10,... | collective-permute-start | bytes 1544 | tf_op jit(solution)/shard_map/ppermute | solution.py:487
  89.3 3.7 %collective-permute-start.4 = (f32[1,128]{1,0:T(1,128)}, f32[1,128]{1,0:T(1,128)S(1)}, u32[]{:S(2)}, u32[]{:S(2)}) collective-permute-start(f32[1,128]{1,0:T(1,128)} %get-tuple-element.29.rest_0_), channel_id=1, source_target_pairs={{0,1},{1,2},{2,3},{3,0},{4,5},{5,6},{6,7},{7,4},{8,9},{9,10},{10,1... | collective-permute-start | bytes 1544 | tf_op jit(solution)/shard_map/ppermute | solution.py:487
  90.0 3.0 %copy-start.13 = (f32[1,128]{1,0:T(1,128)}, f32[1,128]{1,0:T(1,128)S(1)}, u32[]{:S(2)}) copy-start(f32[1,128]{1,0:T(1,128)S(1)} %collective-permute-done.6.rest_3_) | copy-start | bytes 1540
  92.9 0.6 copy-start.14
  93.0 0.6 copy-start.15
  99.3 9.1 %copy-start.16 = (bf16[2048,128]{1,0:T(8,128)(2,1)S(1)}, bf16[2048,128]{1,0:T(8,128)(2,1)}, u32[]{:S(2)}) copy-start(bf16[2048,128]{1,0:T(8,128)(2,1)} %get-tuple-element.32) | copy-start | bytes 1572868
  99.3 39.4 %all-to-all-start.2 = ((bf16[64,64,128]{2,1,0:T(8,128)(2,1)}), bf16[64,64,128]{2,1,0:T(8,128)(2,1)S(1)}, u32[]{:S(2)}, u32[]{:S(2)}) async-start(bf16[64,64,128]{2,1,0:T(8,128)(2,1)} %get-tuple-element.34), calls=%async_computation.2 | async-start | bytes 2097152 | tf_op jit(solution)/shard_map/all_to_all | solution.py:481
  108.4 30.3 %collective-permute-start.7 = (bf16[2048,128]{1,0:T(8,128)(2,1)S(1)}, bf16[2048,128]{1,0:T(8,128)(2,1)S(1)}, u32[]{:S(2)}, u32[]{:S(2)}) collective-permute-start(bf16[2048,128]{1,0:T(8,128)(2,1)S(1)} %copy-done.16), channel_id=1, source_target_pairs={{4,0},{8,4},{12,8},{16,12},{20,16},{24,20},{28,24},{32,28},{36,32}... | collective-permute-start | bytes 1572872 | tf_op jit(solution)/shard_map/ppermute | solution.py:493
  138.7 0.8 copy-start.7
  138.7 1.1 copy-start.5
  146.6 9.2 %copy-start.2 = (bf16[2048,128]{1,0:T(8,128)(2,1)S(1)}, bf16[2048,128]{1,0:T(8,128)(2,1)}, u32[]{:S(2)}) copy-start(bf16[2048,128]{1,0:T(8,128)(2,1)} %key.3) | copy-start | bytes 1572868
  146.6 9.2 %copy-start.3 = (bf16[2048,128]{1,0:T(8,128)(2,1)S(1)}, bf16[2048,128]{1,0:T(8,128)(2,1)}, u32[]{:S(2)}) copy-start(bf16[2048,128]{1,0:T(8,128)(2,1)} %value.3) | copy-start | bytes 1572868
  146.6 9.2 %copy-start.8 = (bf16[2048,128]{1,0:T(8,128)(2,1)S(1)}, bf16[2048,128]{1,0:T(8,128)(2,1)}, u32[]{:S(2)}) copy-start(bf16[2048,128]{1,0:T(8,128)(2,1)} %copy-done.7) | copy-start | bytes 1572868
  146.6 40.5 %all-to-all-start.3 = ((bf16[64,72,128]{2,1,0:T(8,128)(2,1)}), bf16[64,72,128]{2,1,0:T(8,128)(2,1)S(1)}, u32[]{:S(2)}, u32[]{:S(2)}) async-start(bf16[64,72,128]{2,1,0:T(8,128)(2,1)} %filter_grad.1), calls=%async_computation.3 | async-start | bytes 2359296 | tf_op jit(solution)/shard_map/all_to_all | solution.py:481
  187.1 1.1 copy-start.1
where the time goes:
time: 193 us; the launch traced here: 192 us
  waiting for transfers between devices  90.9 us (47%)
  starting transfers between devices  56.2 us (29%)
  Pallas kernels  37.2 us (19%)
  local copies, waits for them, and re-layouts  4.55 us (2%)
  other arithmetic  2.46 us (1%)
    ppermute x2, waiting for transfers between devices, shifted(): return lax.ppermute(block, 'ctx', route)  52.6 us
    all_to_all x4, starting transfers between devices, swapped(): return lax.all_to_all(rows, 'ctx', split_axis=0, concat_axis=0, tiled=True)  42.5 us
    pallas_call x8, Pallas kernels, by_rows(): pl.pallas_call(kernel, grid=(rows // count,), in_specs=in_specs, out_spec...  37.2 us
    all_to_all x4, waiting for transfers between devices, swapped(): return lax.all_to_all(rows, 'ctx', split_axis=0, concat_axis=0, tiled=True)  32 us
    ppermute x6, starting transfers between devices, parts_over_ch(): return [row] + [lax.ppermute(row, 'ch', route) for route in routes]  7.62 us
    ppermute x6, waiting for transfers between devices, parts_over_ch(): return [row] + [lax.ppermute(row, 'ch', route) for route in routes]  6.3 us
    ppermute x2, starting transfers between devices, shifted(): return lax.ppermute(block, 'ctx', route)  6.08 us
    unnamed x34, local copies, waits for them, and re-layouts  4.55 us
  transfers between devices with their start and end apart: 12, of which 9 were waited for; matrix products, arithmetic and copies ran while one was open for 1% of the time, Pallas kernels for 4%

commit v1 on v0

--- a/solution.py
+++ b/solution.py
@@ -81,7 +81,7 @@
     product[...] = (key[...].astype(F32) * value[...].astype(F32)).astype(BF16)
 
 
-def pair_kernel(cotan, filt, unread, pair):
+def pair_kernel(cotan, filt, pair):
     blocks, both = pair.shape[:2]
     pair[:, : both // 2, :] = cotan[...].reshape(blocks, -1, LANES)
     pair[:, both // 2 :, :] = filt[...].astype(BF16).reshape(blocks, -1, LANES)
@@ -98,7 +98,7 @@
 
 
 def mr_forward_kernel(
-    key, value, prior, query, taps, unread, ahead_high, ahead_low, back_high, back_low,
+    key, value, prior, query, taps, ahead_high, ahead_low, back_high, back_low,
     conv_out, mixed_out, window_spec, taps_spec, squares,
 ):
     product = key[...].astype(F32) * value[...].astype(F32)
@@ -138,10 +138,17 @@
     return lax.rsqrt(total(squares) / D + EPSILON)
 
 
-def mr_project_kernel(grad_signal, key_li, mixed, gain, *rest):
-    squares, grad_key_li, project = rest[:-2], rest[-2], rest[-1]
-    grad = grad_signal[...].astype(F32)
-    scaled = mixed[...].astype(F32) * inverse_rms(squares) * gain_block(gain, mixed.shape[0])
+def gate_kernel(mixed, key_li, gain, *rest):
+    squares, signal, inv_out = rest[:-2], rest[-2], rest[-1]
+    inv = inverse_rms(squares)
+    inv_out[...] = inv
+    scaled = mixed[...].astype(F32) * inv * gain_block(gain, mixed.shape[0])
+    signal[...] = (scaled * key_li[...].astype(F32)).astype(BF16)
+
+
+def mr_project_kernel(grad_signal, key_li, mixed, gain, inv_rms, grad_key_li, project):
+    grad = grad_signal[...].reshape(mixed.shape).astype(F32)
+    scaled = mixed[...].astype(F32) * inv_rms[...] * gain_block(gain, mixed.shape[0])
     grad_scaled = grad * scaled
     grad_key_li[...] = grad_scaled.astype(BF16)
 
@@ -153,18 +160,16 @@
 
 
 def mr_backward_kernel(
-    grad_signal, key_li, mixed, conv, query, gain, window_spec, taps_spec,
+    grad_signal, key_li, mixed, conv, query, gain, inv_rms, window_spec, taps_spec,
     ahead_high, ahead_low, back_high, back_low, *rest,
 ):
-    count = (len(rest) - 4) // 2
-    project = total(rest[:count]) / D
-    grad_query, taps_and_signal, before_grad, own_grad = rest[-4:]
-    inv = inverse_rms(rest[count : 2 * count])
+    project = total(rest[:-4]) / D
+    grad_query, taps_grad, before_grad, own_grad = rest[-4:]
+    inv = inv_rms[...]
     normed = mixed[...].astype(F32) * inv
-    gain_col = gain_block(gain, mixed.shape[0])
-    gate = key_li[...].astype(F32)
-    signal = (normed * gain_col * gate).astype(BF16)
-    grad_mixed = inv * (grad_signal[...].astype(F32) * (gate * gain_col) - normed * project)
+    gated = key_li[...].astype(F32) * gain_block(gain, mixed.shape[0])
+    grad = grad_signal[...].reshape(mixed.shape).astype(F32)
+    grad_mixed = inv * (grad * gated - normed * project)
     grad_query[...] = (grad_mixed * conv[...]).astype(BF16)
     grad_conv = grad_mixed * query[...].astype(F32)
     spec = dot2(grad_conv, ahead_high[LANES:], ahead_low[LANES:])
@@ -177,11 +182,7 @@
             axis=1,
         )
 
-    taps_grad = dot1(against(window_spec[...]), back_high[:, :LANES]).astype(BF16)
-    blocks, both_widths = taps_and_signal.shape[:2]
-    width = both_widths // 2
-    taps_and_signal[:, :width, :] = taps_grad.reshape(blocks, width, LANES)
-    taps_and_signal[:, width:, :] = signal.reshape(blocks, width, LANES)
+    taps_grad[...] = dot1(against(window_spec[...]), back_high[:, :LANES]).astype(BF16)
     both = dot1(against(taps_spec[...]), back_high[...])
     before_grad[...] = both[:, :LANES].astype(BF16)
     own_grad[...] = both[:, LANES:]
@@ -192,6 +193,7 @@
 PRODUCT_ROWS = 1024
 PAIR_ROWS = 1024
 FORWARD_ROWS = 1024
+GATE_ROWS = 1024
 PROJECT_ROWS = 1024
 BACKWARD_ROWS = 1024
 
@@ -229,70 +231,110 @@
     )[0]
 
 
-def pair_up(cotan, filt, after, blocks):
+def pair_up(cotan, filt, blocks):
     rows = cotan.shape[0]
     width = rows // blocks
     return by_rows(
         pair_kernel, "pair_up", PAIR_ROWS, rows,
-        (cotan, filt, after), [row_spec(PAIR_ROWS)] * 2 + [UNREAD],
+        (cotan, filt), [row_spec(PAIR_ROWS)] * 2,
         [((blocks, 2 * width, LANES), BF16)],
         [pl.BlockSpec((PAIR_ROWS // width, 2 * width, LANES), lambda i: (i, 0, 0))],
     )[0]
 
 
-def mr_forward(key, value, prior, query, taps, after, tables):
+def mr_forward(key, value, prior, query, taps, tables):
     rows = key.shape[0]
     each, wide = row_spec(FORWARD_ROWS), row_spec(FORWARD_ROWS, 2 * LANES)
     return by_rows(
         mr_forward_kernel, "mr_forward", FORWARD_ROWS, rows,
-        (key, value, prior, query, taps, after, *tables),
-        [each] * 5 + [UNREAD] + [whole_spec(table.shape) for table in tables],
+        (key, value, prior, query, taps, *tables),
+        [each] * 5 + [whole_spec(table.shape) for table in tables],
         [((rows, LANES), F32), ((rows, LANES), BF16)] + [((rows, 2 * LANES), F32)] * 2 + [ROW],
         [each, each, wide, wide, whole_spec((1, LANES))],
     )
 
 
-def mr_project(grad_signal, key_li, mixed, gain, squares):
+def gate(mixed, key_li, gain, squares):
+    rows = mixed.shape[0]
+    each = row_spec(GATE_ROWS)
+    return by_rows(
+        gate_kernel, "gate", GATE_ROWS, rows,
+        (mixed, key_li, gain, *squares),
+        [each] * 2 + [whole_spec(gain.shape)] + [whole_spec((1, LANES))] * len(squares),
+        [((rows, LANES), BF16), ROW],
+        [each, whole_spec((1, LANES))],
+    )
+
+
+def first_half_spec(pair, count):
+    width = pair.shape[1] // 2
+    return pl.BlockSpec((count // width, width, LANES), lambda i: (i, 0, 0))
+
+
+def mr_project(moved, key_li, mixed, gain, inv_rms):
     rows = mixed.shape[0]
     each = row_spec(PROJECT_ROWS)
     return by_rows(
         mr_project_kernel, "mr_project", PROJECT_ROWS, rows,
-        (grad_signal, key_li, mixed, gain, *squares),
-        [each] * 3 + [whole_spec(gain.shape)] + [whole_spec((1, LANES))] * len(squares),
+        (moved, key_li, mixed, gain, inv_rms),
+        [first_half_spec(moved, PROJECT_ROWS)]
+        + [each] * 2
+        + [whole_spec(gain.shape), whole_spec((1, LANES))],
         [((rows, LANES), BF16), ROW],
         [each, whole_spec((1, LANES))],
     )
 
 
 def mr_backward(
-    grad_signal, key_li, mixed, conv, query, gain, window_spec, taps_spec, tables, project,
-    squares, blocks,
+    moved, key_li, mixed, conv, query, gain, inv_rms, window_spec, taps_spec, tables, project
 ):
     rows = mixed.shape[0]
-    width = rows // blocks
     each, wide = row_spec(BACKWARD_ROWS), row_spec(BACKWARD_ROWS, 2 * LANES)
     return by_rows(
         mr_backward_kernel, "mr_backward", BACKWARD_ROWS, rows,
         (
-            grad_signal, key_li, mixed, conv, query, gain, window_spec, taps_spec,
-            *tables, *project, *squares,
+            moved, key_li, mixed, conv, query, gain, inv_rms, window_spec, taps_spec,
+            *tables, *project,
         ),
-        [each] * 5
-        + [whole_spec(gain.shape)]
+        [first_half_spec(moved, BACKWARD_ROWS)]
+        + [each] * 4
+        + [whole_spec(gain.shape), whole_spec((1, LANES))]
         + [wide] * 2
         + [whole_spec(table.shape) for table in tables]
-        + [whole_spec((1, LANES))] * (len(project) + len(squares)),
-        [
-            ((rows, LANES), BF16), ((blocks, 2 * width, LANES), BF16), ((rows, LANES), BF16),
-            ((rows, LANES), F32),
-        ],
-        [
-            each,
-            pl.BlockSpec((BACKWARD_ROWS // width, 2 * width, LANES), lambda i: (i, 0, 0)),
-            each,
-            each,
-        ],
-    )
+        + [whole_spec((1, LANES))] * len(project),
+        [((rows, LANES), BF16)] * 3 + [((rows, LANES), F32)],
+        [each] * 4,
+    )
+
+
+def hold(values, after):
+    return pl.pallas_call(
+        lambda *refs: None,
+        in_specs=[UNREAD] * 2,
+        out_specs=UNREAD,
+        out_shape=jax.ShapeDtypeStruct(values.shape, values.dtype),
+        input_output_aliases={0: 0},
+        name="hold",
+    )(values, after)
+
+
+def bundle_kernel(bundled, taps_grad, unread, out):
+    taps = jnp.sum(taps_grad[...].astype(F32), axis=0).astype(BF16)
+    out[...] = jnp.broadcast_to(taps[None], out.shape)
+
+
+def bundle(bundled, taps_grad, after):
+    whole = taps_grad.shape
+    return pl.pallas_call(
+        bundle_kernel,
+        grid=(1,),
+        in_specs=[UNREAD, whole_spec(whole), UNREAD],
+        out_specs=pl.BlockSpec(whole, lambda i: (0, 1, 0)),
+        out_shape=jax.ShapeDtypeStruct(bundled.shape, bundled.dtype),
+        input_output_aliases={0: 0},
+        compiler_params=LIMIT,
+        name="bundle",
+    )(bundled, taps_grad, after)
 
 
 def deliver_kernel(bundled, gain, filter_grad, taps_grad, gain_grad):
@@ -322,7 +364,7 @@
 
 
 def deliver(bundled, gain, blocks, width):
-    each = min(16, blocks)
+    each = min(32, blocks)
     rows = row_spec(each * width)
     return by_rows(
         deliver_kernel, "deliver", each, blocks,
@@ -337,7 +379,7 @@
 
 
 EXTRA = 8
-GROUP = 8
+GROUP = 16
 
 
 def channel_rows(channel, blocks, width):
@@ -382,9 +424,10 @@
 
 
 def signal_grad_kernel(
-    blocks, width, pair, unread, first, cosine, sine, second, second_back, last,
-    grad_out, cotan_spec, pair_flat, grad_flat,
+    blocks, width, pair, signal, first, cosine, sine, second, second_back, last,
+    outward, cotan_spec, pair_flat, grad_flat,
 ):
+    outward[:, width:, :] = signal[...].reshape(blocks, width, LANES)
     pair_flat[...] = pair[...].astype(F32)
 
     def one_group(step, carry):
@@ -407,17 +450,16 @@
         return carry
 
     lax.fori_loop(0, width // GROUP, one_group, 0)
-    grad_out[...] = grad_flat[...].astype(BF16)
+    outward[:, :width, :] = grad_flat[...].astype(BF16).reshape(blocks, width, LANES)
 
 
 def filter_grad_kernel(
-    blocks, width, together, moved, cotan_spec, grad_signal, unread, first, cosine, sine, second,
-    second_back, last, bundled, moved_flat, grad_flat,
+    blocks, width, together, signal, cotan_spec, grad_signal, unread, first, cosine, sine, second,
+    second_back, last, bundled, signal_flat, grad_flat,
 ):
-    moved_flat[...] = moved[...].reshape(moved_flat.shape).astype(F32)
-    taps = jnp.sum(moved[:, :width, :].astype(F32), axis=0).astype(BF16)
-    bundled[:, width : 2 * width, :] = jnp.broadcast_to(taps[None], (blocks, width, LANES))
-    terms = moved[:, width:, :].astype(F32) * grad_signal[...].astype(F32)
+    values = signal[...].astype(F32)
+    signal_flat[...] = values.reshape(signal_flat.shape)
+    terms = values * grad_signal[...].astype(F32)
     sums = jnp.sum(jnp.sum(terms, axis=0), axis=1, keepdims=True)
     high = sums.astype(BF16).astype(F32)
     place = lax.broadcasted_iota(jnp.int32, (width, LANES), 0)
@@ -433,7 +475,7 @@
     def one_group(step, carry):
         channels = [step * GROUP + at for at in range(GROUP)]
         spec = to_spectrum(
-            moved_flat, channels, blocks, 2 * width, width, first, cosine, sine, second
+            signal_flat, channels, blocks, width, 0, first, cosine, sine, second
         )
         rows = pl.ds(pl.multiple_of(step * (GROUP * blocks), GROUP * blocks), GROUP * blocks)
         grads = from_spectrum(
@@ -448,32 +490,38 @@
     bundled[:, :width, :] = grad_flat[...].reshape(blocks, width, LANES).astype(BF16)
 
 
-def signal_grad(pair, after, blocks, tables):
+def signal_grad(pair, signal, blocks, tables):
     rows = pair.shape[0] // 2
-    return by_rows(
-        functools.partial(signal_grad_kernel, blocks, rows // blocks), "signal_grad", 1, 1,
-        (pair, after, *tables),
-        [whole_spec(pair.shape), UNREAD] + [whole_spec(table.shape) for table in tables],
-        [((rows, LANES), BF16), ((rows, 2 * LANES), F32)],
-        [whole_spec((rows, LANES)), whole_spec((rows, 2 * LANES))],
+    width = rows // blocks
+    shape = (blocks, 2 * width, LANES)
+    ins = (pair, signal, *tables)
+    return by_rows(
+        functools.partial(signal_grad_kernel, blocks, width), "signal_grad", 1, 1,
+        ins, [whole_spec(value.shape) for value in ins],
+        [(shape, BF16), ((rows, 2 * LANES), F32)],
+        [whole_spec(shape), whole_spec((rows, 2 * LANES))],
         [pltpu.VMEM((2 * rows, LANES), F32), pltpu.VMEM((rows, LANES), F32)],
     )
 
 
-def filter_grad(moved, cotan_spec, grad_signal, after, tables):
+def filter_grad(moved, cotan_spec, outward, after, tables):
     blocks, both, _ = moved.shape
     width = both // 2
-    ins = (moved, cotan_spec, grad_signal.reshape(blocks, width, LANES))
+    half = (blocks, width, LANES)
     shape = (blocks, 2 * width + EXTRA, LANES)
     return by_rows(
         functools.partial(filter_grad_kernel, blocks, width, LANES // width), "filter_grad", 1, 1,
-        (*ins, after, *tables),
-        [whole_spec(value.shape) for value in ins]
-        + [UNREAD]
+        (moved, cotan_spec, outward, after, *tables),
+        [
+            pl.BlockSpec(half, lambda i: (0, 1, 0)),
+            whole_spec(cotan_spec.shape),
+            whole_spec(half),
+            UNREAD,
+        ]
         + [whole_spec(table.shape) for table in tables],
         [(shape, BF16)],
         [whole_spec(shape)],
-        [pltpu.VMEM((2 * blocks * width, LANES), F32), pltpu.VMEM((blocks * width, LANES), F32)],
+        [pltpu.VMEM((blocks * width, LANES), F32)] * 2,
     )[0]
 
 
@@ -500,26 +548,28 @@
     long = long_tables(blocks)
     width = rows // blocks
     gain = norm_gain.reshape(-1, LANES)
-    product = product_of(key_mr, value_mr)
-    prior = shifted(product, 1)
-    pair = pair_up(cotangent, filter_li, product, blocks)
+    prior = shifted(product_of(key_mr, value_mr), 1)
+    pair = hold(pair_up(cotangent, filter_li, blocks), prior)
     moved_pair = swapped(pair).reshape(2 * rows, LANES)
-    grad_moved, cotan_spec = signal_grad(moved_pair, prior, blocks, long)
-    grad_signal = swapped(grad_moved)
     conv, mixed, window_spec, taps_spec, squares = mr_forward(
-        key_mr, value_mr, prior, query_mr, filter_mr, grad_moved, short
-    )
-    squares = parts_over_ch(squares)
-    grad_key_li, terms = mr_project(grad_signal, key_li, mixed, gain, squares)
-    grad_query, taps_and_signal, before_grad, own_grad = mr_backward(
-        grad_signal, key_li, mixed, conv, query_mr, gain, window_spec, taps_spec, short,
-        parts_over_ch(terms), squares, blocks,
+        key_mr, value_mr, prior, query_mr, filter_mr, short
+    )
+    signal, inv_rms = gate(mixed, key_li, gain, parts_over_ch(squares))
+    outward, cotan_spec = signal_grad(moved_pair, signal, blocks, long)
+    moved = swapped(outward)
+    grad_key_li, terms = mr_project(moved, key_li, mixed, gain, inv_rms)
+    grad_query, taps_grad, before_grad, own_grad = mr_backward(
+        moved, key_li, mixed, conv, query_mr, gain, inv_rms, window_spec, taps_spec, short,
+        parts_over_ch(terms),
     )
     after = shifted(before_grad, -1)
     grad_product = own_grad + after.astype(F32)
     grad_key = (grad_product * value_mr.astype(F32)).astype(BF16)
     grad_value = (grad_product * key_mr.astype(F32)).astype(BF16)
-    bundled = filter_grad(swapped(taps_and_signal), cotan_spec, grad_moved, after, long)
+    moved_taps = swapped(taps_grad).reshape(blocks, width, LANES)
+    bundled = bundle(
+        filter_grad(moved, cotan_spec, outward, taps_grad, long), moved_taps, after
+    )
     grad_filter_li, grad_filter_mr, gain_rows = deliver(swapped(bundled), gain, blocks, width)
     grad_gain = gain_rows.reshape(rows)
     return (

time: 193 us -> 190 us (0.984)
  blocking collectives: 0 us -> 34.9 us
  waiting for transfers between devices: 90.9 us -> 61.5 us
  starting transfers between devices: 56.2 us -> 45.7 us
    ppermute x2, waiting for transfers between devices: 52.6 us -> 15.3 us  [shifted(): return lax.ppermute(block, 'ctx', route)]
    all_to_all x0 -> x1, blocking collectives: none -> 34.9 us  [swapped(): return lax.all_to_all(rows, 'ctx', split_axis=0, concat_axis=0, tiled=True)]
    all_to_all x4 -> x3, starting transfers between devices: 42.5 us -> 30.7 us  [swapped(): return lax.all_to_all(rows, 'ctx', split_axis=0, concat_axis=0, tiled=True)]
    all_to_all x4 -> x3, waiting for transfers between devices: 32 us -> 39.9 us  [swapped(): return lax.all_to_all(rows, 'ctx', split_axis=0, concat_axis=0, tiled=True)]
    pallas_call x0 -> x2, Pallas kernels: none -> 1.99 us  [the longest x1 1.99 us: bundle(): pl.pallas_call(bundle_kernel, grid=(1,), in_specs=[UNREAD, whole_spec(who...]
    pallas_call x8 -> x9, Pallas kernels: 37.2 us -> 36.2 us  [by_rows(): pl.pallas_call(kernel, grid=(rows // count,), in_specs=in_specs, out_spec...]
    unnamed x34 -> x28, local copies, waits for them, and re-layouts: 4.55 us -> 5.47 us
  transfers between devices with their start and end apart: 12 -> 11, of which waited for: 9 -> 8; matrix products, arithmetic and copies ran while one was open for 1% -> 1% of each run, Pallas kernels for 4% -> 9%
where the time goes in v1:
time: 190 us; the launch traced here: 189 us
  waiting for transfers between devices  61.5 us (32%)
  starting transfers between devices  45.7 us (24%)
  Pallas kernels  38.1 us (20%)
  blocking collectives  34.9 us (18%)
  local copies, waits for them, and re-layouts  5.47 us (3%)
  other arithmetic  2.47 us (1%)
    all_to_all x3, waiting for transfers between devices, swapped(): return lax.all_to_all(rows, 'ctx', split_axis=0, concat_axis=0, tiled=True)  39.9 us
    pallas_call x9, Pallas kernels, by_rows(): pl.pallas_call(kernel, grid=(rows // count,), in_specs=in_specs, out_spec...  36.2 us
    all_to_all x1, blocking collectives, swapped(): return lax.all_to_all(rows, 'ctx', split_axis=0, concat_axis=0, tiled=True)  34.9 us
    all_to_all x3, starting transfers between devices, swapped(): return lax.all_to_all(rows, 'ctx', split_axis=0, concat_axis=0, tiled=True)  30.7 us
    ppermute x2, waiting for transfers between devices, shifted(): return lax.ppermute(block, 'ctx', route)  15.3 us
    ppermute x6, starting transfers between devices, parts_over_ch(): return [row] + [lax.ppermute(row, 'ch', route) for route in routes]  7.64 us
    ppermute x2, starting transfers between devices, shifted(): return lax.ppermute(block, 'ctx', route)  7.29 us
    ppermute x6, waiting for transfers between devices, parts_over_ch(): return [row] + [lax.ppermute(row, 'ch', route) for route in routes]  6.37 us
  transfers between devices with their start and end apart: 11, of which 8 were waited for; matrix products, arithmetic and copies ran while one was open for 1% of the time, Pallas kernels for 9%

profile of v1, /device:TPU:1, one launch (start us, length us, event | category | flops | bytes accessed | tf_op | source)
XLA Modules:
  0.0 188.8 jit_solution(3832261347221069404)
XLA Ops:
  0.6 2.0 %product_of.1 = bf16[2048,128]{1,0:T(8,128)(2,1)} custom-call(bf16[2048,128]{1,0:T(8,128)(2,1)} %key.3, bf16[2048,128]{1,0:T(8,128)(2,1)} %value.3), custom_call_target="tpu_custom_call" | custom-call | tf_op jit(solution)/shard_map/product_of/pallas_call | solution.py:210
  2.6 4.9 %collective-permute-start = (bf16[2048,128]{1,0:T(8,128)(2,1)}, bf16[2048,128]{1,0:T(8,128)(2,1)S(1)}, u32[]{:S(2)}, u32[]{:S(2)}) collective-permute-start(bf16[2048,128]{1,0:T(8,128)(2,1)} %product_of.1), channel_id=1, source_target_pairs={{0,4},{4,8},{8,12},{12,16},{16,20},{20,24},{24,28},{28,32},{32,36}... | collective-permute-start | bytes 1572872 | tf_op jit(solution)/shard_map/ppermute | solution.py:541
  7.5 2.2 %pair_up.1.refs_0_ = bf16[64,64,128]{2,1,0:T(8,128)(2,1)} custom-call(bf16[2048,128]{1,0:T(8,128)(2,1)} %cotan.1, f32[2048,128]{1,0:T(8,128)} %filt.1), custom_call_target="tpu_custom_call" | custom-call | tf_op jit(solution)/shard_map/pair_up/pallas_call | solution.py:210
  9.7 4.2 %collective-permute-done.refs_1_.prior = bf16[2048,128]{1,0:T(8,128)(2,1)S(1)} collective-permute-done((bf16[2048,128]{1,0:T(8,128)(2,1)}, bf16[2048,128]{1,0:T(8,128)(2,1)S(1)}, u32[]{:S(2)}, u32[]{:S(2)}) %collective-permute-start) | collective-permute-done | bytes 524320 | tf_op jit(solution)/shard_map/ppermute | solution.py:541
  14.0 0.8 copy-done.4
  14.7 13.5 %all-to-all-start = ((bf16[64,64,128]{2,1,0:T(8,128)(2,1)}), bf16[64,64,128]{2,1,0:T(8,128)(2,1)S(1)}, u32[]{:S(2)}, u32[]{:S(2)}) async-start(bf16[64,64,128]{2,1,0:T(8,128)(2,1)} %hold.1), calls=%async_computation | async-start | bytes 2097152 | tf_op jit(solution)/shard_map/all_to_all | solution.py:529
  28.3 7.3 %mr_forward.1 = (f32[2048,128]{1,0:T(8,128)}, bf16[2048,128]{1,0:T(8,128)(2,1)}, f32[2048,256]{1,0:T(8,128)}, f32[2048,256]{1,0:T(8,128)}, f32[1,128]{1,0:T(1,128)}) custom-call(bf16[2048,128]{1,0:T(8,128)(2,1)} %key.3, bf16[2048,128]{1,0:T(8,128)(2,1)} %value.3, bf16[2048,128]{1,0:T(8,128)(2,1)} %copy-done.4, bf16[2048,128]{1,0:T(8,128)(2,1)} %query.3, ...), custom_call_target="tpu_custom_call" | custom-call | tf_op jit(solution)/shard_map/mr_forward/pallas_call | solution.py:210
  35.6 2.8 %collective-permute-start.3 = (f32[1,128]{1,0:T(1,128)}, f32[1,128]{1,0:T(1,128)S(1)}, u32[]{:S(2)}, u32[]{:S(2)}) collective-permute-start(f32[1,128]{1,0:T(1,128)} %get-tuple-element.26.rest_0_), channel_id=1, source_target_pairs={{0,3},{1,0},{2,1},{3,2},{4,7},{5,4},{6,5},{7,6},{8,11},{9,8},{10,9... | collective-permute-start | bytes 1544 | tf_op jit(solution)/shard_map/ppermute | solution.py:535
  38.8 0.7 collective-permute-start.1
  39.5 3.3 %collective-permute-done.2.rest_2_ = f32[1,128]{1,0:T(1,128)S(1)} collective-permute-done((f32[1,128]{1,0:T(1,128)}, f32[1,128]{1,0:T(1,128)S(1)}, u32[]{:S(2)}, u32[]{:S(2)}) %collective-permute-start.2) | collective-permute-done | bytes 544 | tf_op jit(solution)/shard_map/ppermute | solution.py:535
  43.3 2.5 %gate.1 = (bf16[2048,128]{1,0:T(8,128)(2,1)}, f32[1,128]{1,0:T(1,128)}) custom-call(bf16[2048,128]{1,0:T(8,128)(2,1)} %get-tuple-element.25.mixed, bf16[2048,128]{1,0:T(8,128)(2,1)} %key_li.5, f32[16,128]{1,0:T(8,128)} %bitcast.6, f32[1,128]{1,0:T(1,128)} %get-tuple-element.26.rest_0_, f32[1,128]{1,0:T(1,128)} %copy-done.13, f32[1,128]{1,0:T(1,128)} %copy-done.12, ...), custom_call_target="tpu_custom_call" | custom-call | tf_op jit(solution)/shard_map/gate/pallas_call | solution.py:210
  45.8 11.0 %all-to-all-done = bf16[64,64,128]{2,1,0:T(8,128)(2,1)S(1)} async-done(((bf16[64,64,128]{2,1,0:T(8,128)(2,1)}), bf16[64,64,128]{2,1,0:T(8,128)(2,1)S(1)}, u32[]{:S(2)}, u32[]{:S(2)}) %all-to-all-start) | async-done | bytes 1048608 | tf_op jit(solution)/shard_map/all_to_all | solution.py:529
  56.9 1.0 copy-done.3
  57.8 5.9 %signal_grad.1 = (bf16[64,64,128]{2,1,0:T(8,128)(2,1)}, f32[2048,256]{1,0:T(8,128)}) custom-call(bf16[4096,128]{1,0:T(8,128)(2,1)} %bitcast.4, bf16[2048,128]{1,0:T(8,128)(2,1)} %get-tuple-element.27.signal, bf16[128,128]{1,0:T(8,128)(2,1)} %constant.36.first, f32[64,128]{1,0:T(8,128)} %constant.32.clone.cosine, f32[64,128]{1,0:T(8,128)} %constant.33.clone.sine, ...), custom_call_target="tpu_custom_call" | custom-call | tf_op jit(solution)/shard_map/signal_grad/pallas_call | solution.py:210
  63.8 34.9 %all_to_all.24.grad_signal.signal = bf16[64,64,128]{2,1,0:T(8,128)(2,1)} all-to-all(bf16[64,64,128]{2,1,0:T(8,128)(2,1)} %get-tuple-element.28.grad_signal), channel_id=1, replica_groups=mesh['ctx'=64,'ch'=4] {'ctx'}, dimensions={0} | all-to-all | bytes 2097152 | tf_op jit(solution)/shard_map/all_to_all | solution.py:529
  98.6 2.8 %mr_project.1 = (bf16[2048,128]{1,0:T(8,128)(2,1)}, f32[1,128]{1,0:T(1,128)}) custom-call(bf16[64,64,128]{2,1,0:T(8,128)(2,1)} %all_to_all.24.grad_signal.signal, bf16[2048,128]{1,0:T(8,128)(2,1)} %key_li.5, bf16[2048,128]{1,0:T(8,128)(2,1)} %get-tuple-element.25.mixed, f32[16,128]{1,0:T(8,128)} %bitcast.7, f32[1,128]{1,0:T(1,128)} %get-tuple-element.30.inv_rms), custom_call_target="tpu_custom_call" | custom-call | tf_op jit(solution)/shard_map/mr_project/pallas_call | solution.py:210
  101.4 2.8 %collective-permute-start.6 = (f32[1,128]{1,0:T(1,128)}, f32[1,128]{1,0:T(1,128)S(1)}, u32[]{:S(2)}, u32[]{:S(2)}) collective-permute-start(f32[1,128]{1,0:T(1,128)} %get-tuple-element.33.rest_0_), channel_id=1, source_target_pairs={{0,3},{1,0},{2,1},{3,2},{4,7},{5,4},{6,5},{7,6},{8,11},{9,8},{10,9... | collective-permute-start | bytes 1544 | tf_op jit(solution)/shard_map/ppermute | solution.py:535
  104.5 0.7 collective-permute-start.4
  105.2 3.0 %collective-permute-done.5.rest_2_ = f32[1,128]{1,0:T(1,128)S(1)} collective-permute-done((f32[1,128]{1,0:T(1,128)}, f32[1,128]{1,0:T(1,128)S(1)}, u32[]{:S(2)}, u32[]{:S(2)}) %collective-permute-start.5) | collective-permute-done | bytes 544 | tf_op jit(solution)/shard_map/ppermute | solution.py:535
  108.8 5.2 %mr_backward.1 = (bf16[2048,128]{1,0:T(8,128)(2,1)}, bf16[2048,128]{1,0:T(8,128)(2,1)}, bf16[2048,128]{1,0:T(8,128)(2,1)}, f32[2048,128]{1,0:T(8,128)}) custom-call(bf16[64,64,128]{2,1,0:T(8,128)(2,1)} %all_to_all.24.grad_signal.signal, bf16[2048,128]{1,0:T(8,128)(2,1)} %key_li.5, bf16[2048,128]{1,0:T(8,128)(2,1)} %get-tuple-element.25.mixed, ...), custom_call_target="tpu_custom_call" | custom-call | tf_op jit(solution)/shard_map/mr_backward/pallas_call | solution.py:210
  114.0 8.1 %all-to-all-start.2 = ((bf16[64,32,128]{2,1,0:T(8,128)(2,1)}), bf16[64,32,128]{2,1,0:T(8,128)(2,1)S(1)}, u32[]{:S(2)}, u32[]{:S(2)}) async-start(bf16[64,32,128]{2,1,0:T(8,128)(2,1)} %bitcast.5), calls=%async_computation.2 | async-start | bytes 1048576 | tf_op jit(solution)/shard_map/all_to_all | solution.py:529
  122.1 2.4 %collective-permute-start.7 = (bf16[2048,128]{1,0:T(8,128)(2,1)}, bf16[2048,128]{1,0:T(8,128)(2,1)S(1)}, u32[]{:S(2)}, u32[]{:S(2)}) collective-permute-start(bf16[2048,128]{1,0:T(8,128)(2,1)} %get-tuple-element.36), channel_id=1, source_target_pairs={{4,0},{8,4},{12,8},{16,12},{20,16},{24,20},{28,24},{32,28},{36,32}... | collective-permute-start | bytes 1572872 | tf_op jit(solution)/shard_map/ppermute | solution.py:541
  124.5 5.6 %filter_grad.1.bundled = bf16[64,72,128]{2,1,0:T(8,128)(2,1)} custom-call(bf16[64,64,128]{2,1,0:T(8,128)(2,1)} %all_to_all.24.grad_signal.signal, f32[2048,256]{1,0:T(8,128)} %get-tuple-element.38.cotan_spec, bf16[64,64,128]{2,1,0:T(8,128)(2,1)} %get-tuple-element.28.grad_signal, bf16[2048,128]{1,0:T(8,128)(2,1)} %get-tuple-element.39.unread, ...), custom_call_target="tpu_custom_call" | custom-call | tf_op jit(solution)/shard_map/filter_grad/pallas_call | solution.py:210
  130.1 11.1 %collective-permute-done.7.unread = bf16[2048,128]{1,0:T(8,128)(2,1)S(1)} collective-permute-done((bf16[2048,128]{1,0:T(8,128)(2,1)}, bf16[2048,128]{1,0:T(8,128)(2,1)S(1)}, u32[]{:S(2)}, u32[]{:S(2)}) %collective-permute-start.7) | collective-permute-done | bytes 524320 | tf_op jit(solution)/shard_map/ppermute | solution.py:541
  141.1 0.8 copy-done.5
  141.9 0.8 copy-done.7
  142.7 2.0 %bundle.1 = bf16[64,72,128]{2,1,0:T(8,128)(2,1)} custom-call(bf16[64,72,128]{2,1,0:T(8,128)(2,1)} %filter_grad.1.bundled, bf16[64,32,128]{2,1,0:T(8,128)(2,1)} %copy-done.7, bf16[2048,128]{1,0:T(8,128)(2,1)} %copy-done.5), custom_call_target="tpu_custom_call", output_to_operand_aliasing={{}: (0, {})} | custom-call | tf_op jit(solution)/shard_map/bundle/pallas_call | solution.py:328
  144.7 9.1 %all-to-all-start.3 = ((bf16[64,72,128]{2,1,0:T(8,128)(2,1)}), bf16[64,72,128]{2,1,0:T(8,128)(2,1)S(1)}, u32[]{:S(2)}, u32[]{:S(2)}) async-start(bf16[64,72,128]{2,1,0:T(8,128)(2,1)} %bundle.1), calls=%async_computation.3 | async-start | bytes 2359296 | tf_op jit(solution)/shard_map/all_to_all | solution.py:529
  153.9 2.5 %multiply_convert_fusion = (bf16[2048,128]{1,0:T(8,128)(2,1)}, bf16[2048,128]{1,0:T(8,128)(2,1)}) fusion(bf16[2048,128]{1,0:T(8,128)(2,1)S(1)} %copy-done, f32[2048,128]{1,0:T(8,128)} %get-tuple-element.35, bf16[2048,128]{1,0:T(8,128)(2,1)S(1)} %copy-done.6, bf16[2048,128]{1,0:T(8,128)(2,1)S(1)} %copy-done.1), kind=kLoop, calls=%fused_computation | loop fusion | flops 2097152 | bytes 3670016 | tf_op jit(solution)/shard_map/convert_element_type | solution.py:568
  156.3 28.9 %all-to-all-done.3.bundled = bf16[64,72,128]{2,1,0:T(8,128)(2,1)S(1)} async-done(((bf16[64,72,128]{2,1,0:T(8,128)(2,1)}), bf16[64,72,128]{2,1,0:T(8,128)(2,1)S(1)}, u32[]{:S(2)}, u32[]{:S(2)}) %all-to-all-start.3) | async-done | bytes 1179680 | tf_op jit(solution)/shard_map/all_to_all | solution.py:529
  185.2 1.0 copy-done.2
  186.2 2.6 %deliver.1 = (f32[2048,128]{1,0:T(8,128)}, f32[2048,128]{1,0:T(8,128)}, f32[16,128]{1,0:T(8,128)}) custom-call(bf16[64,72,128]{2,1,0:T(8,128)(2,1)} %copy-done.2, f32[16,128]{1,0:T(8,128)} %bitcast.9), custom_call_target="tpu_custom_call" | custom-call | tf_op jit(solution)/shard_map/deliver/pallas_call | solution.py:210
  (31 shorter events, 1.9 us)
Async XLA Ops:
  2.6 11.4 %collective-permute-start = (bf16[2048,128]{1,0:T(8,128)(2,1)}, bf16[2048,128]{1,0:T(8,128)(2,1)S(1)}, u32[]{:S(2)}, u32[]{:S(2)}) collective-permute-start(bf16[2048,128]{1,0:T(8,128)(2,1)} %product_of.1), channel_id=1, source_target_pairs={{0,4},{4,8},{8,12},{12,16},{16,20},{20,24},{24,28},{28,32},{32,36}... | collective-permute-start | bytes 1572872 | tf_op jit(solution)/shard_map/ppermute | solution.py:541
  14.0 0.8 copy-start.4
  14.7 42.1 %all-to-all-start = ((bf16[64,64,128]{2,1,0:T(8,128)(2,1)}), bf16[64,64,128]{2,1,0:T(8,128)(2,1)S(1)}, u32[]{:S(2)}, u32[]{:S(2)}) async-start(bf16[64,64,128]{2,1,0:T(8,128)(2,1)} %hold.1), calls=%async_computation | async-start | bytes 2097152 | tf_op jit(solution)/shard_map/all_to_all | solution.py:529
  35.6 3.9 %collective-permute-start.3 = (f32[1,128]{1,0:T(1,128)}, f32[1,128]{1,0:T(1,128)S(1)}, u32[]{:S(2)}, u32[]{:S(2)}) collective-permute-start(f32[1,128]{1,0:T(1,128)} %get-tuple-element.26.rest_0_), channel_id=1, source_target_pairs={{0,3},{1,0},{2,1},{3,2},{4,7},{5,4},{6,5},{7,6},{8,11},{9,8},{10,9... | collective-permute-start | bytes 1544 | tf_op jit(solution)/shard_map/ppermute | solution.py:535
  38.4 4.3 %collective-permute-start.2 = (f32[1,128]{1,0:T(1,128)}, f32[1,128]{1,0:T(1,128)S(1)}, u32[]{:S(2)}, u32[]{:S(2)}) collective-permute-start(f32[1,128]{1,0:T(1,128)} %get-tuple-element.26.rest_0_), channel_id=1, source_target_pairs={{0,2},{1,3},{2,0},{3,1},{4,6},{5,7},{6,4},{7,5},{8,10},{9,11},{10,... | collective-permute-start | bytes 1544 | tf_op jit(solution)/shard_map/ppermute | solution.py:535
  38.8 4.0 %collective-permute-start.1 = (f32[1,128]{1,0:T(1,128)}, f32[1,128]{1,0:T(1,128)S(1)}, u32[]{:S(2)}, u32[]{:S(2)}) collective-permute-start(f32[1,128]{1,0:T(1,128)} %get-tuple-element.26.rest_0_), channel_id=1, source_target_pairs={{0,1},{1,2},{2,3},{3,0},{4,5},{5,6},{6,7},{7,4},{8,9},{9,10},{10,1... | collective-permute-start | bytes 1544 | tf_op jit(solution)/shard_map/ppermute | solution.py:535
  39.5 3.3 %copy-start.11 = (f32[1,128]{1,0:T(1,128)}, f32[1,128]{1,0:T(1,128)S(1)}, u32[]{:S(2)}) copy-start(f32[1,128]{1,0:T(1,128)S(1)} %collective-permute-done.3.rest_3_) | copy-start | bytes 1540
  42.7 0.5 copy-start.12
  42.8 0.5 copy-start.13
  56.9 1.0 copy-start.3
  101.4 3.8 %collective-permute-start.6 = (f32[1,128]{1,0:T(1,128)}, f32[1,128]{1,0:T(1,128)S(1)}, u32[]{:S(2)}, u32[]{:S(2)}) collective-permute-start(f32[1,128]{1,0:T(1,128)} %get-tuple-element.33.rest_0_), channel_id=1, source_target_pairs={{0,3},{1,0},{2,1},{3,2},{4,7},{5,4},{6,5},{7,6},{8,11},{9,8},{10,9... | collective-permute-start | bytes 1544 | tf_op jit(solution)/shard_map/ppermute | solution.py:535
  104.1 4.0 %collective-permute-start.5 = (f32[1,128]{1,0:T(1,128)}, f32[1,128]{1,0:T(1,128)S(1)}, u32[]{:S(2)}, u32[]{:S(2)}) collective-permute-start(f32[1,128]{1,0:T(1,128)} %get-tuple-element.33.rest_0_), channel_id=1, source_target_pairs={{0,2},{1,3},{2,0},{3,1},{4,6},{5,7},{6,4},{7,5},{8,10},{9,11},{10,... | collective-permute-start | bytes 1544 | tf_op jit(solution)/shard_map/ppermute | solution.py:535
  104.5 3.7 %collective-permute-start.4 = (f32[1,128]{1,0:T(1,128)}, f32[1,128]{1,0:T(1,128)S(1)}, u32[]{:S(2)}, u32[]{:S(2)}) collective-permute-start(f32[1,128]{1,0:T(1,128)} %get-tuple-element.33.rest_0_), channel_id=1, source_target_pairs={{0,1},{1,2},{2,3},{3,0},{4,5},{5,6},{6,7},{7,4},{8,9},{9,10},{10,1... | collective-permute-start | bytes 1544 | tf_op jit(solution)/shard_map/ppermute | solution.py:535
  105.2 3.0 %copy-start.8 = (f32[1,128]{1,0:T(1,128)}, f32[1,128]{1,0:T(1,128)S(1)}, u32[]{:S(2)}) copy-start(f32[1,128]{1,0:T(1,128)S(1)} %collective-permute-done.6.rest_3_) | copy-start | bytes 1540
  108.1 0.5 copy-start.9
  108.2 0.6 copy-start.10
  114.0 27.1 %all-to-all-start.2 = ((bf16[64,32,128]{2,1,0:T(8,128)(2,1)}), bf16[64,32,128]{2,1,0:T(8,128)(2,1)S(1)}, u32[]{:S(2)}, u32[]{:S(2)}) async-start(bf16[64,32,128]{2,1,0:T(8,128)(2,1)} %bitcast.5), calls=%async_computation.2 | async-start | bytes 1048576 | tf_op jit(solution)/shard_map/all_to_all | solution.py:529
  122.1 19.0 %collective-permute-start.7 = (bf16[2048,128]{1,0:T(8,128)(2,1)}, bf16[2048,128]{1,0:T(8,128)(2,1)S(1)}, u32[]{:S(2)}, u32[]{:S(2)}) collective-permute-start(bf16[2048,128]{1,0:T(8,128)(2,1)} %get-tuple-element.36), channel_id=1, source_target_pairs={{4,0},{8,4},{12,8},{16,12},{20,16},{24,20},{28,24},{32,28},{36,32}... | collective-permute-start | bytes 1572872 | tf_op jit(solution)/shard_map/ppermute | solution.py:541
  130.1 23.8 %copy-start = (bf16[2048,128]{1,0:T(8,128)(2,1)S(1)}, bf16[2048,128]{1,0:T(8,128)(2,1)}, u32[]{:S(2)}) copy-start(bf16[2048,128]{1,0:T(8,128)(2,1)} %key.3) | copy-start | bytes 1572868
  130.1 23.8 %copy-start.1 = (bf16[2048,128]{1,0:T(8,128)(2,1)S(1)}, bf16[2048,128]{1,0:T(8,128)(2,1)}, u32[]{:S(2)}) copy-start(bf16[2048,128]{1,0:T(8,128)(2,1)} %value.3) | copy-start | bytes 1572868
  141.1 0.8 copy-start.5
  141.9 0.8 copy-start.7
  144.7 9.2 %copy-start.6 = (bf16[2048,128]{1,0:T(8,128)(2,1)S(1)}, bf16[2048,128]{1,0:T(8,128)(2,1)}, u32[]{:S(2)}) copy-start(bf16[2048,128]{1,0:T(8,128)(2,1)} %copy-done.5) | copy-start | bytes 1572868
  144.7 40.5 %all-to-all-start.3 = ((bf16[64,72,128]{2,1,0:T(8,128)(2,1)}), bf16[64,72,128]{2,1,0:T(8,128)(2,1)S(1)}, u32[]{:S(2)}, u32[]{:S(2)}) async-start(bf16[64,72,128]{2,1,0:T(8,128)(2,1)} %bundle.1), calls=%async_computation.3 | async-start | bytes 2359296 | tf_op jit(solution)/shard_map/all_to_all | solution.py:529
  185.2 1.0 copy-start.2

commit v2 on v0

--- a/solution.py
+++ b/solution.py
@@ -81,7 +81,7 @@
     product[...] = (key[...].astype(F32) * value[...].astype(F32)).astype(BF16)
 
 
-def pair_kernel(cotan, filt, unread, pair):
+def pair_kernel(cotan, filt, pair):
     blocks, both = pair.shape[:2]
     pair[:, : both // 2, :] = cotan[...].reshape(blocks, -1, LANES)
     pair[:, both // 2 :, :] = filt[...].astype(BF16).reshape(blocks, -1, LANES)
@@ -152,37 +152,52 @@
     project[...] += jnp.sum(grad_scaled * key_li[...].astype(F32), axis=0, keepdims=True)
 
 
-def mr_backward_kernel(
-    grad_signal, key_li, mixed, conv, query, gain, window_spec, taps_spec,
-    ahead_high, ahead_low, back_high, back_low, *rest,
-):
-    count = (len(rest) - 4) // 2
-    project = total(rest[:count]) / D
-    grad_query, taps_and_signal, before_grad, own_grad = rest[-4:]
-    inv = inverse_rms(rest[count : 2 * count])
+def against(spec, other):
+    spec_re, spec_im = spec[:, :LANES], spec[:, LANES:]
+    other_re, other_im = other[:, :LANES], other[:, LANES:]
+    return jnp.concatenate(
+        [spec_re * other_re + spec_im * other_im, spec_im * other_re - spec_re * other_im], axis=1
+    )
+
+
+def mixed_gradient(grad_signal, key_li, mixed, gain, project, squares):
+    inv = inverse_rms(squares)
     normed = mixed[...].astype(F32) * inv
-    gain_col = gain_block(gain, mixed.shape[0])
-    gate = key_li[...].astype(F32)
-    signal = (normed * gain_col * gate).astype(BF16)
-    grad_mixed = inv * (grad_signal[...].astype(F32) * (gate * gain_col) - normed * project)
-    grad_query[...] = (grad_mixed * conv[...]).astype(BF16)
-    grad_conv = grad_mixed * query[...].astype(F32)
-    spec = dot2(grad_conv, ahead_high[LANES:], ahead_low[LANES:])
-    spec_re, spec_im = spec[:, :LANES], spec[:, LANES:]
-
-    def against(other):
-        other_re, other_im = other[:, :LANES], other[:, LANES:]
-        return jnp.concatenate(
-            [spec_re * other_re + spec_im * other_im, spec_im * other_re - spec_re * other_im],
-            axis=1,
-        )
-
-    taps_grad = dot1(against(window_spec[...]), back_high[:, :LANES]).astype(BF16)
+    gated = key_li[...].astype(F32) * gain_block(gain, mixed.shape[0])
+    grads = grad_signal[...].astype(F32) * gated - normed * (total(project) / D)
+    return inv * grads, normed * gated
+
+
+def taps_grad_kernel(
+    grad_signal, key_li, mixed, query, gain, window_spec,
+    ahead_high, ahead_low, back_high, *rest,
+):
+    count = (len(rest) - 2) // 2
+    taps_and_signal, spec_out = rest[-2:]
+    grad_mixed, signal = mixed_gradient(
+        grad_signal, key_li, mixed, gain, rest[:count], rest[count : 2 * count]
+    )
+    spec = dot2(
+        grad_mixed * query[...].astype(F32), ahead_high[LANES:], ahead_low[LANES:]
+    )
+    spec_out[...] = spec
+    taps_grad = dot1(against(spec, window_spec[...]), back_high[:, :LANES]).astype(BF16)
     blocks, both_widths = taps_and_signal.shape[:2]
     width = both_widths // 2
     taps_and_signal[:, :width, :] = taps_grad.reshape(blocks, width, LANES)
-    taps_and_signal[:, width:, :] = signal.reshape(blocks, width, LANES)
-    both = dot1(against(taps_spec[...]), back_high[...])
+    taps_and_signal[:, width:, :] = signal.astype(BF16).reshape(blocks, width, LANES)
+
+
+def product_grad_kernel(
+    grad_signal, key_li, mixed, conv, gain, spec, taps_spec, back_high, *rest
+):
+    count = (len(rest) - 3) // 2
+    grad_query, before_grad, own_grad = rest[-3:]
+    grad_mixed, _ = mixed_gradient(
+        grad_signal, key_li, mixed, gain, rest[:count], rest[count : 2 * count]
+    )
+    grad_query[...] = (grad_mixed * conv[...]).astype(BF16)
+    both = dot1(against(spec[...], taps_spec[...]), back_high[...])
     before_grad[...] = both[:, :LANES].astype(BF16)
     own_grad[...] = both[:, LANES:]
 
@@ -229,12 +244,12 @@
     )[0]
 
 
-def pair_up(cotan, filt, after, blocks):
+def pair_up(cotan, filt, blocks):
     rows = cotan.shape[0]
     width = rows // blocks
     return by_rows(
         pair_kernel, "pair_up", PAIR_ROWS, rows,
-        (cotan, filt, after), [row_spec(PAIR_ROWS)] * 2 + [UNREAD],
+        (cotan, filt), [row_spec(PAIR_ROWS)] * 2,
         [((blocks, 2 * width, LANES), BF16)],
         [pl.BlockSpec((PAIR_ROWS // width, 2 * width, LANES), lambda i: (i, 0, 0))],
     )[0]
@@ -264,34 +279,40 @@
     )
 
 
-def mr_backward(
-    grad_signal, key_li, mixed, conv, query, gain, window_spec, taps_spec, tables, project,
-    squares, blocks,
+def taps_grad_of(
+    grad_signal, key_li, mixed, query, gain, window_spec, tables, project, squares, blocks
 ):
     rows = mixed.shape[0]
     width = rows // blocks
     each, wide = row_spec(BACKWARD_ROWS), row_spec(BACKWARD_ROWS, 2 * LANES)
     return by_rows(
-        mr_backward_kernel, "mr_backward", BACKWARD_ROWS, rows,
+        taps_grad_kernel, "taps_grad_of", BACKWARD_ROWS, rows,
+        (grad_signal, key_li, mixed, query, gain, window_spec, *tables[:3], *project, *squares),
+        [each] * 4
+        + [whole_spec(gain.shape), wide]
+        + [whole_spec(table.shape) for table in tables[:3]]
+        + [whole_spec((1, LANES))] * (len(project) + len(squares)),
+        [((blocks, 2 * width, LANES), BF16), ((rows, 2 * LANES), F32)],
+        [pl.BlockSpec((BACKWARD_ROWS // width, 2 * width, LANES), lambda i: (i, 0, 0)), wide],
+    )
+
+
+def product_grad_of(
+    grad_signal, key_li, mixed, conv, gain, spec, taps_spec, tables, project, squares
+):
+    rows = mixed.shape[0]
+    each, wide = row_spec(BACKWARD_ROWS), row_spec(BACKWARD_ROWS, 2 * LANES)
+    return by_rows(
+        product_grad_kernel, "product_grad_of", BACKWARD_ROWS, rows,
         (
-            grad_signal, key_li, mixed, conv, query, gain, window_spec, taps_spec,
-            *tables, *project, *squares,
+            grad_signal, key_li, mixed, conv, gain, spec, taps_spec, tables[2],
+            *project, *squares,
         ),
-        [each] * 5
-        + [whole_spec(gain.shape)]
-        + [wide] * 2
-        + [whole_spec(table.shape) for table in tables]
+        [each] * 4
+        + [whole_spec(gain.shape), wide, wide, whole_spec(tables[2].shape)]
         + [whole_spec((1, LANES))] * (len(project) + len(squares)),
-        [
-            ((rows, LANES), BF16), ((blocks, 2 * width, LANES), BF16), ((rows, LANES), BF16),
-            ((rows, LANES), F32),
-        ],
-        [
-            each,
-            pl.BlockSpec((BACKWARD_ROWS // width, 2 * width, LANES), lambda i: (i, 0, 0)),
-            each,
-            each,
-        ],
+        [((rows, LANES), BF16)] * 2 + [((rows, LANES), F32)],
+        [each] * 3,
     )
 
 
@@ -322,7 +343,7 @@
 
 
 def deliver(bundled, gain, blocks, width):
-    each = min(16, blocks)
+    each = min(32, blocks)
     rows = row_spec(each * width)
     return by_rows(
         deliver_kernel, "deliver", each, blocks,
@@ -337,7 +358,7 @@
 
 
 EXTRA = 8
-GROUP = 8
+GROUP = 16
 
 
 def channel_rows(channel, blocks, width):
@@ -500,10 +521,8 @@
     long = long_tables(blocks)
     width = rows // blocks
     gain = norm_gain.reshape(-1, LANES)
-    product = product_of(key_mr, value_mr)
-    prior = shifted(product, 1)
-    pair = pair_up(cotangent, filter_li, product, blocks)
-    moved_pair = swapped(pair).reshape(2 * rows, LANES)
+    moved_pair = swapped(pair_up(cotangent, filter_li, blocks)).reshape(2 * rows, LANES)
+    prior = shifted(product_of(key_mr, value_mr), 1)
     grad_moved, cotan_spec = signal_grad(moved_pair, prior, blocks, long)
     grad_signal = swapped(grad_moved)
     conv, mixed, window_spec, taps_spec, squares = mr_forward(
@@ -511,15 +530,19 @@
     )
     squares = parts_over_ch(squares)
     grad_key_li, terms = mr_project(grad_signal, key_li, mixed, gain, squares)
-    grad_query, taps_and_signal, before_grad, own_grad = mr_backward(
-        grad_signal, key_li, mixed, conv, query_mr, gain, window_spec, taps_spec, short,
-        parts_over_ch(terms), squares, blocks,
+    project = parts_over_ch(terms)
+    taps_and_signal, spec = taps_grad_of(
+        grad_signal, key_li, mixed, query_mr, gain, window_spec, short, project, squares, blocks
+    )
+    moved = swapped(taps_and_signal)
+    grad_query, before_grad, own_grad = product_grad_of(
+        grad_signal, key_li, mixed, conv, gain, spec, taps_spec, short, project, squares
     )
     after = shifted(before_grad, -1)
     grad_product = own_grad + after.astype(F32)
     grad_key = (grad_product * value_mr.astype(F32)).astype(BF16)
     grad_value = (grad_product * key_mr.astype(F32)).astype(BF16)
-    bundled = filter_grad(swapped(taps_and_signal), cotan_spec, grad_moved, after, long)
+    bundled = filter_grad(moved, cotan_spec, grad_moved, after, long)
     grad_filter_li, grad_filter_mr, gain_rows = deliver(swapped(bundled), gain, blocks, width)
     grad_gain = gain_rows.reshape(rows)
     return (

time: 193 us -> 186 us (0.964)
  waiting for transfers between devices: 90.9 us -> 84.8 us
    ppermute x2, waiting for transfers between devices: 52.6 us -> 46.4 us  [shifted(): return lax.ppermute(block, 'ctx', route)]
    pallas_call x8 -> x9, Pallas kernels: 37.2 us -> 37.4 us  [by_rows(): pl.pallas_call(kernel, grid=(rows // count,), in_specs=in_specs, out_spec...]
    unnamed x34 -> x30, local copies, waits for them, and re-layouts: 4.55 us -> 4.47 us
  transfers between devices with their start and end apart: 12 -> 12, of which waited for: 9 -> 9; matrix products, arithmetic and copies ran while one was open for 1% -> 1% of each run, Pallas kernels for 4% -> 7%
where the time goes in v2:
time: 186 us; the launch traced here: 185 us
  waiting for transfers between devices  84.8 us (46%)
  starting transfers between devices  55.5 us (30%)
  Pallas kernels  37.4 us (20%)
  local copies, waits for them, and re-layouts  4.47 us (2%)
  other arithmetic  2.46 us (1%)
    ppermute x2, waiting for transfers between devices, shifted(): return lax.ppermute(block, 'ctx', route)  46.4 us
    all_to_all x4, starting transfers between devices, swapped(): return lax.all_to_all(rows, 'ctx', split_axis=0, concat_axis=0, tiled=True)  42 us
    pallas_call x9, Pallas kernels, by_rows(): pl.pallas_call(kernel, grid=(rows // count,), in_specs=in_specs, out_spec...  37.4 us
    all_to_all x4, waiting for transfers between devices, swapped(): return lax.all_to_all(rows, 'ctx', split_axis=0, concat_axis=0, tiled=True)  31.9 us
    ppermute x6, starting transfers between devices, parts_over_ch(): return [row] + [lax.ppermute(row, 'ch', route) for route in routes]  7.63 us
    ppermute x6, waiting for transfers between devices, parts_over_ch(): return [row] + [lax.ppermute(row, 'ch', route) for route in routes]  6.45 us
    ppermute x2, starting transfers between devices, shifted(): return lax.ppermute(block, 'ctx', route)  5.89 us
    unnamed x30, local copies, waits for them, and re-layouts  4.47 us
  transfers between devices with their start and end apart: 12, of which 9 were waited for; matrix products, arithmetic and copies ran while one was open for 1% of the time, Pallas kernels for 7%

profile of v2, /device:TPU:1, one launch (start us, length us, event | category | flops | bytes accessed | tf_op | source)
XLA Modules:
  0.0 185.4 jit_solution(17360890414035719416)
XLA Ops:
  0.6 2.2 %pair_up.1 = bf16[64,64,128]{2,1,0:T(8,128)(2,1)} custom-call(bf16[2048,128]{1,0:T(8,128)(2,1)} %cotan.1, f32[2048,128]{1,0:T(8,128)} %filt.1), custom_call_target="tpu_custom_call" | custom-call | tf_op jit(solution)/shard_map/pair_up/pallas_call | solution.py:223
  2.8 13.0 %all-to-all-start = ((bf16[64,64,128]{2,1,0:T(8,128)(2,1)}), bf16[64,64,128]{2,1,0:T(8,128)(2,1)S(1)}, u32[]{:S(2)}, u32[]{:S(2)}) async-start(bf16[64,64,128]{2,1,0:T(8,128)(2,1)} %pair_up.1), calls=%async_computation | async-start | bytes 2097152 | tf_op jit(solution)/shard_map/all_to_all | solution.py:502
  15.8 2.0 %product_of.1 = bf16[2048,128]{1,0:T(8,128)(2,1)} custom-call(bf16[2048,128]{1,0:T(8,128)(2,1)} %key.3, bf16[2048,128]{1,0:T(8,128)(2,1)} %value.3), custom_call_target="tpu_custom_call" | custom-call | tf_op jit(solution)/shard_map/product_of/pallas_call | solution.py:223
  17.8 3.5 %collective-permute-start = (bf16[2048,128]{1,0:T(8,128)(2,1)}, bf16[2048,128]{1,0:T(8,128)(2,1)S(1)}, u32[]{:S(2)}, u32[]{:S(2)}) collective-permute-start(bf16[2048,128]{1,0:T(8,128)(2,1)} %product_of.1), channel_id=1, source_target_pairs={{0,4},{4,8},{8,12},{12,16},{16,20},{20,24},{24,28},{28,32},{32,36}... | collective-permute-start | bytes 1572872 | tf_op jit(solution)/shard_map/ppermute | solution.py:514
  21.3 23.0 %collective-permute-done.unread.prior = bf16[2048,128]{1,0:T(8,128)(2,1)S(1)} collective-permute-done((bf16[2048,128]{1,0:T(8,128)(2,1)}, bf16[2048,128]{1,0:T(8,128)(2,1)S(1)}, u32[]{:S(2)}, u32[]{:S(2)}) %collective-permute-start) | collective-permute-done | bytes 524320 | tf_op jit(solution)/shard_map/ppermute | solution.py:514
  44.6 0.6 copy-done.8
  45.2 0.4 copy-done.4
  45.6 5.6 %signal_grad.1 = (bf16[2048,128]{1,0:T(8,128)(2,1)}, f32[2048,256]{1,0:T(8,128)}) custom-call(bf16[4096,128]{1,0:T(8,128)(2,1)} %bitcast.10, bf16[2048,128]{1,0:T(8,128)(2,1)} %copy-done.8, bf16[128,128]{1,0:T(8,128)(2,1)} %constant.36.first, f32[64,128]{1,0:T(8,128)} %constant.32.clone.cosine, f32[64,128]{1,0:T(8,128)} %constant.33.clone.sine, ...), custom_call_target="tpu_custom_call" | custom-call | tf_op jit(solution)/shard_map/signal_grad/pallas_call | solution.py:223
  51.2 11.2 %all-to-all-start.1 = ((bf16[64,32,128]{2,1,0:T(8,128)(2,1)}), bf16[64,32,128]{2,1,0:T(8,128)(2,1)S(1)}, u32[]{:S(2)}, u32[]{:S(2)}) async-start(bf16[64,32,128]{2,1,0:T(8,128)(2,1)} %bitcast.8), calls=%async_computation.1 | async-start | bytes 1048576 | tf_op jit(solution)/shard_map/all_to_all | solution.py:502
  62.4 7.3 %mr_forward.1 = (f32[2048,128]{1,0:T(8,128)}, bf16[2048,128]{1,0:T(8,128)(2,1)}, f32[2048,256]{1,0:T(8,128)}, f32[2048,256]{1,0:T(8,128)}, f32[1,128]{1,0:T(1,128)}) custom-call(bf16[2048,128]{1,0:T(8,128)(2,1)} %key.3, bf16[2048,128]{1,0:T(8,128)(2,1)} %value.3, bf16[2048,128]{1,0:T(8,128)(2,1)} %copy-done.8, bf16[2048,128]{1,0:T(8,128)(2,1)} %query.3, ...), custom_call_target="tpu_custom_call" | custom-call | tf_op jit(solution)/shard_map/mr_forward/pallas_call | solution.py:223
  69.7 2.8 %collective-permute-start.3 = (f32[1,128]{1,0:T(1,128)}, f32[1,128]{1,0:T(1,128)S(1)}, u32[]{:S(2)}, u32[]{:S(2)}) collective-permute-start(f32[1,128]{1,0:T(1,128)} %get-tuple-element.28.rest_0_.rest_4_), channel_id=1, source_target_pairs={{0,3},{1,0},{2,1},{3,2},{4,7},{5,4},{6,5},{7,6},{8,11},{9,8},{10,9... | collective-permute-start | bytes 1544 | tf_op jit(solution)/shard_map/ppermute | solution.py:508
  72.9 0.7 collective-permute-start.1
  73.6 3.3 %collective-permute-done.2.rest_2_.rest_6_ = f32[1,128]{1,0:T(1,128)S(1)} collective-permute-done((f32[1,128]{1,0:T(1,128)}, f32[1,128]{1,0:T(1,128)S(1)}, u32[]{:S(2)}, u32[]{:S(2)}) %collective-permute-start.2) | collective-permute-done | bytes 544 | tf_op jit(solution)/shard_map/ppermute | solution.py:508
  76.9 2.8 %all-to-all-done.1 = bf16[64,32,128]{2,1,0:T(8,128)(2,1)S(1)} async-done(((bf16[64,32,128]{2,1,0:T(8,128)(2,1)}), bf16[64,32,128]{2,1,0:T(8,128)(2,1)S(1)}, u32[]{:S(2)}, u32[]{:S(2)}) %all-to-all-start.1) | async-done | bytes 524320 | tf_op jit(solution)/shard_map/all_to_all | solution.py:502
  79.8 0.8 copy-done
  80.5 2.8 %mr_project.1 = (bf16[2048,128]{1,0:T(8,128)(2,1)}, f32[1,128]{1,0:T(1,128)}) custom-call(bf16[2048,128]{1,0:T(8,128)(2,1)} %bitcast.5, bf16[2048,128]{1,0:T(8,128)(2,1)} %key_li.5, bf16[2048,128]{1,0:T(8,128)(2,1)} %get-tuple-element.25.mixed, f32[16,128]{1,0:T(8,128)} %bitcast.11, f32[1,128]{1,0:T(1,128)} %get-tuple-element.28.rest_0_.rest_4_, ...), custom_call_target="tpu_custom_call" | custom-call | tf_op jit(solution)/shard_map/mr_project/pallas_call | solution.py:223
  83.3 2.7 %collective-permute-start.6 = (f32[1,128]{1,0:T(1,128)}, f32[1,128]{1,0:T(1,128)S(1)}, u32[]{:S(2)}, u32[]{:S(2)}) collective-permute-start(f32[1,128]{1,0:T(1,128)} %get-tuple-element.29.rest_0_), channel_id=1, source_target_pairs={{0,3},{1,0},{2,1},{3,2},{4,7},{5,4},{6,5},{7,6},{8,11},{9,8},{10,9... | collective-permute-start | bytes 1544 | tf_op jit(solution)/shard_map/ppermute | solution.py:508
  86.4 0.7 collective-permute-start.4
  87.1 3.1 %collective-permute-done.5.rest_2_ = f32[1,128]{1,0:T(1,128)S(1)} collective-permute-done((f32[1,128]{1,0:T(1,128)}, f32[1,128]{1,0:T(1,128)S(1)}, u32[]{:S(2)}, u32[]{:S(2)}) %collective-permute-start.5) | collective-permute-done | bytes 544 | tf_op jit(solution)/shard_map/ppermute | solution.py:508
  90.2 0.4 copy-done.13
  90.7 4.5 %taps_grad_of.1 = (bf16[64,64,128]{2,1,0:T(8,128)(2,1)}, f32[2048,256]{1,0:T(8,128)}) custom-call(bf16[2048,128]{1,0:T(8,128)(2,1)} %bitcast.6, bf16[2048,128]{1,0:T(8,128)(2,1)} %key_li.5, bf16[2048,128]{1,0:T(8,128)(2,1)} %get-tuple-element.25.mixed, bf16[2048,128]{1,0:T(8,128)(2,1)} %query.3, f32[16,128]{1,0:T(8,128)} %bitcast.12, ...), custom_call_target="tpu_custom_call" | custom-call | tf_op jit(solution)/shard_map/taps_grad_of/pallas_call | solution.py:223
  95.2 8.7 %all-to-all-start.2 = ((bf16[64,64,128]{2,1,0:T(8,128)(2,1)}), bf16[64,64,128]{2,1,0:T(8,128)(2,1)S(1)}, u32[]{:S(2)}, u32[]{:S(2)}) async-start(bf16[64,64,128]{2,1,0:T(8,128)(2,1)} %get-tuple-element.36), calls=%async_computation.2 | async-start | bytes 2097152 | tf_op jit(solution)/shard_map/all_to_all | solution.py:502
  103.9 4.5 %product_grad_of.1 = (bf16[2048,128]{1,0:T(8,128)(2,1)}, bf16[2048,128]{1,0:T(8,128)(2,1)}, f32[2048,128]{1,0:T(8,128)}) custom-call(bf16[2048,128]{1,0:T(8,128)(2,1)} %bitcast.7, bf16[2048,128]{1,0:T(8,128)(2,1)} %key_li.5, bf16[2048,128]{1,0:T(8,128)(2,1)} %get-tuple-element.25.mixed, f32[2048,128]{1,0:T(8,128)} %get-tuple-element.26.conv, ...), custom_call_target="tpu_custom_call" | custom-call | tf_op jit(solution)/shard_map/product_grad_of/pallas_call | solution.py:223
  108.4 2.4 %collective-permute-start.7 = (bf16[2048,128]{1,0:T(8,128)(2,1)}, bf16[2048,128]{1,0:T(8,128)(2,1)S(1)}, u32[]{:S(2)}, u32[]{:S(2)}) collective-permute-start(bf16[2048,128]{1,0:T(8,128)(2,1)} %get-tuple-element.34), channel_id=1, source_target_pairs={{4,0},{8,4},{12,8},{16,12},{20,16},{24,20},{28,24},{32,28},{36,32}... | collective-permute-start | bytes 1572872 | tf_op jit(solution)/shard_map/ppermute | solution.py:514
  110.8 23.4 %collective-permute-done.7.unread = bf16[2048,128]{1,0:T(8,128)(2,1)S(1)} collective-permute-done((bf16[2048,128]{1,0:T(8,128)(2,1)}, bf16[2048,128]{1,0:T(8,128)(2,1)S(1)}, u32[]{:S(2)}, u32[]{:S(2)}) %collective-permute-start.7) | collective-permute-done | bytes 524320 | tf_op jit(solution)/shard_map/ppermute | solution.py:514
  134.2 0.8 copy-done.6
  135.3 5.9 %filter_grad.1 = bf16[64,72,128]{2,1,0:T(8,128)(2,1)} custom-call(bf16[64,64,128]{2,1,0:T(8,128)(2,1)} %copy-done.5, f32[2048,256]{1,0:T(8,128)} %get-tuple-element.37.cotan_spec, bf16[64,32,128]{2,1,0:T(8,128)(2,1)} %bitcast.9, bf16[2048,128]{1,0:T(8,128)(2,1)} %copy-done.6, bf16[128,128]{1,0:T(8,128)(2,1)} %constant.36.first, ...), custom_call_target="tpu_custom_call" | custom-call | tf_op jit(solution)/shard_map/filter_grad/pallas_call | solution.py:223
  141.2 9.1 %all-to-all-start.3 = ((bf16[64,72,128]{2,1,0:T(8,128)(2,1)}), bf16[64,72,128]{2,1,0:T(8,128)(2,1)S(1)}, u32[]{:S(2)}, u32[]{:S(2)}) async-start(bf16[64,72,128]{2,1,0:T(8,128)(2,1)} %filter_grad.1), calls=%async_computation.3 | async-start | bytes 2359296 | tf_op jit(solution)/shard_map/all_to_all | solution.py:502
  150.4 2.5 %multiply_convert_fusion = (bf16[2048,128]{1,0:T(8,128)(2,1)}, bf16[2048,128]{1,0:T(8,128)(2,1)}) fusion(bf16[2048,128]{1,0:T(8,128)(2,1)S(1)} %copy-done.2, f32[2048,128]{1,0:T(8,128)} %get-tuple-element.33, bf16[2048,128]{1,0:T(8,128)(2,1)S(1)} %copy-done.7, bf16[2048,128]{1,0:T(8,128)(2,1)S(1)} %copy-done.3), kind=kLoop, calls=%fused_computation | loop fusion | flops 2097152 | bytes 3670016 | tf_op jit(solution)/shard_map/convert_element_type | solution.py:544
  152.8 28.9 %all-to-all-done.3.bundled = bf16[64,72,128]{2,1,0:T(8,128)(2,1)S(1)} async-done(((bf16[64,72,128]{2,1,0:T(8,128)(2,1)}), bf16[64,72,128]{2,1,0:T(8,128)(2,1)S(1)}, u32[]{:S(2)}, u32[]{:S(2)}) %all-to-all-start.3) | async-done | bytes 1179680 | tf_op jit(solution)/shard_map/all_to_all | solution.py:502
  181.7 1.0 copy-done.1
  182.8 2.6 %deliver.1 = (f32[2048,128]{1,0:T(8,128)}, f32[2048,128]{1,0:T(8,128)}, f32[16,128]{1,0:T(8,128)}) custom-call(bf16[64,72,128]{2,1,0:T(8,128)(2,1)} %copy-done.1, f32[16,128]{1,0:T(8,128)} %bitcast.14), custom_call_target="tpu_custom_call" | custom-call | tf_op jit(solution)/shard_map/deliver/pallas_call | solution.py:223
  (32 shorter events, 1.5 us)
Async XLA Ops:
  2.8 41.7 %all-to-all-start = ((bf16[64,64,128]{2,1,0:T(8,128)(2,1)}), bf16[64,64,128]{2,1,0:T(8,128)(2,1)S(1)}, u32[]{:S(2)}, u32[]{:S(2)}) async-start(bf16[64,64,128]{2,1,0:T(8,128)(2,1)} %pair_up.1), calls=%async_computation | async-start | bytes 2097152 | tf_op jit(solution)/shard_map/all_to_all | solution.py:502
  17.8 26.6 %collective-permute-start = (bf16[2048,128]{1,0:T(8,128)(2,1)}, bf16[2048,128]{1,0:T(8,128)(2,1)S(1)}, u32[]{:S(2)}, u32[]{:S(2)}) collective-permute-start(bf16[2048,128]{1,0:T(8,128)(2,1)} %product_of.1), channel_id=1, source_target_pairs={{0,4},{4,8},{8,12},{12,16},{16,20},{20,24},{24,28},{28,32},{32,36}... | collective-permute-start | bytes 1572872 | tf_op jit(solution)/shard_map/ppermute | solution.py:514
  44.4 0.8 copy-start.8
  44.6 1.0 copy-start.4
  51.2 28.6 %all-to-all-start.1 = ((bf16[64,32,128]{2,1,0:T(8,128)(2,1)}), bf16[64,32,128]{2,1,0:T(8,128)(2,1)S(1)}, u32[]{:S(2)}, u32[]{:S(2)}) async-start(bf16[64,32,128]{2,1,0:T(8,128)(2,1)} %bitcast.8), calls=%async_computation.1 | async-start | bytes 1048576 | tf_op jit(solution)/shard_map/all_to_all | solution.py:502
  69.7 3.9 %collective-permute-start.3 = (f32[1,128]{1,0:T(1,128)}, f32[1,128]{1,0:T(1,128)S(1)}, u32[]{:S(2)}, u32[]{:S(2)}) collective-permute-start(f32[1,128]{1,0:T(1,128)} %get-tuple-element.28.rest_0_.rest_4_), channel_id=1, source_target_pairs={{0,3},{1,0},{2,1},{3,2},{4,7},{5,4},{6,5},{7,6},{8,11},{9,8},{10,9... | collective-permute-start | bytes 1544 | tf_op jit(solution)/shard_map/ppermute | solution.py:508
  72.5 4.3 %collective-permute-start.2 = (f32[1,128]{1,0:T(1,128)}, f32[1,128]{1,0:T(1,128)S(1)}, u32[]{:S(2)}, u32[]{:S(2)}) collective-permute-start(f32[1,128]{1,0:T(1,128)} %get-tuple-element.28.rest_0_.rest_4_), channel_id=1, source_target_pairs={{0,2},{1,3},{2,0},{3,1},{4,6},{5,7},{6,4},{7,5},{8,10},{9,11},{10,... | collective-permute-start | bytes 1544 | tf_op jit(solution)/shard_map/ppermute | solution.py:508
  72.9 4.0 %collective-permute-start.1 = (f32[1,128]{1,0:T(1,128)}, f32[1,128]{1,0:T(1,128)S(1)}, u32[]{:S(2)}, u32[]{:S(2)}) collective-permute-start(f32[1,128]{1,0:T(1,128)} %get-tuple-element.28.rest_0_.rest_4_), channel_id=1, source_target_pairs={{0,1},{1,2},{2,3},{3,0},{4,5},{5,6},{6,7},{7,4},{8,9},{9,10},{10,1... | collective-permute-start | bytes 1544 | tf_op jit(solution)/shard_map/ppermute | solution.py:508
  73.6 6.2 %copy-start.9 = (f32[1,128]{1,0:T(1,128)}, f32[1,128]{1,0:T(1,128)S(1)}, u32[]{:S(2)}) copy-start(f32[1,128]{1,0:T(1,128)S(1)} %collective-permute-done.3.rest_3_.rest_7_) | copy-start | bytes 1540
  76.8 2.9 %copy-start.10 = (f32[1,128]{1,0:T(1,128)}, f32[1,128]{1,0:T(1,128)S(1)}, u32[]{:S(2)}) copy-start(f32[1,128]{1,0:T(1,128)S(1)} %collective-permute-done.2.rest_2_.rest_6_) | copy-start | bytes 1540
  76.9 2.9 %copy-start.11 = (f32[1,128]{1,0:T(1,128)}, f32[1,128]{1,0:T(1,128)S(1)}, u32[]{:S(2)}) copy-start(f32[1,128]{1,0:T(1,128)S(1)} %collective-permute-done.1.rest_1_.rest_5_) | copy-start | bytes 1540
  79.7 0.8 copy-start
  83.3 3.8 %collective-permute-start.6 = (f32[1,128]{1,0:T(1,128)}, f32[1,128]{1,0:T(1,128)S(1)}, u32[]{:S(2)}, u32[]{:S(2)}) collective-permute-start(f32[1,128]{1,0:T(1,128)} %get-tuple-element.29.rest_0_), channel_id=1, source_target_pairs={{0,3},{1,0},{2,1},{3,2},{4,7},{5,4},{6,5},{7,6},{8,11},{9,8},{10,9... | collective-permute-start | bytes 1544 | tf_op jit(solution)/shard_map/ppermute | solution.py:508
  86.0 4.1 %collective-permute-start.5 = (f32[1,128]{1,0:T(1,128)}, f32[1,128]{1,0:T(1,128)S(1)}, u32[]{:S(2)}, u32[]{:S(2)}) collective-permute-start(f32[1,128]{1,0:T(1,128)} %get-tuple-element.29.rest_0_), channel_id=1, source_target_pairs={{0,2},{1,3},{2,0},{3,1},{4,6},{5,7},{6,4},{7,5},{8,10},{9,11},{10,... | collective-permute-start | bytes 1544 | tf_op jit(solution)/shard_map/ppermute | solution.py:508
  86.4 3.8 %collective-permute-start.4 = (f32[1,128]{1,0:T(1,128)}, f32[1,128]{1,0:T(1,128)S(1)}, u32[]{:S(2)}, u32[]{:S(2)}) collective-permute-start(f32[1,128]{1,0:T(1,128)} %get-tuple-element.29.rest_0_), channel_id=1, source_target_pairs={{0,1},{1,2},{2,3},{3,0},{4,5},{5,6},{6,7},{7,4},{8,9},{9,10},{10,1... | collective-permute-start | bytes 1544 | tf_op jit(solution)/shard_map/ppermute | solution.py:508
  87.1 3.1 %copy-start.12 = (f32[1,128]{1,0:T(1,128)}, f32[1,128]{1,0:T(1,128)S(1)}, u32[]{:S(2)}) copy-start(f32[1,128]{1,0:T(1,128)S(1)} %collective-permute-done.6.rest_3_) | copy-start | bytes 1540
  90.2 0.5 copy-start.13
  90.2 0.5 copy-start.14
  95.2 38.9 %all-to-all-start.2 = ((bf16[64,64,128]{2,1,0:T(8,128)(2,1)}), bf16[64,64,128]{2,1,0:T(8,128)(2,1)S(1)}, u32[]{:S(2)}, u32[]{:S(2)}) async-start(bf16[64,64,128]{2,1,0:T(8,128)(2,1)} %get-tuple-element.36), calls=%async_computation.2 | async-start | bytes 2097152 | tf_op jit(solution)/shard_map/all_to_all | solution.py:502
  108.4 25.7 %collective-permute-start.7 = (bf16[2048,128]{1,0:T(8,128)(2,1)}, bf16[2048,128]{1,0:T(8,128)(2,1)S(1)}, u32[]{:S(2)}, u32[]{:S(2)}) collective-permute-start(bf16[2048,128]{1,0:T(8,128)(2,1)} %get-tuple-element.34), channel_id=1, source_target_pairs={{4,0},{8,4},{12,8},{16,12},{20,16},{24,20},{28,24},{32,28},{36,32}... | collective-permute-start | bytes 1572872 | tf_op jit(solution)/shard_map/ppermute | solution.py:514
  134.2 0.8 copy-start.6
  134.2 1.1 copy-start.5
  141.2 9.1 %copy-start.2 = (bf16[2048,128]{1,0:T(8,128)(2,1)S(1)}, bf16[2048,128]{1,0:T(8,128)(2,1)}, u32[]{:S(2)}) copy-start(bf16[2048,128]{1,0:T(8,128)(2,1)} %key.3) | copy-start | bytes 1572868
  141.2 9.2 %copy-start.3 = (bf16[2048,128]{1,0:T(8,128)(2,1)S(1)}, bf16[2048,128]{1,0:T(8,128)(2,1)}, u32[]{:S(2)}) copy-start(bf16[2048,128]{1,0:T(8,128)(2,1)} %value.3) | copy-start | bytes 1572868
  141.2 9.2 %copy-start.7 = (bf16[2048,128]{1,0:T(8,128)(2,1)S(1)}, bf16[2048,128]{1,0:T(8,128)(2,1)}, u32[]{:S(2)}) copy-start(bf16[2048,128]{1,0:T(8,128)(2,1)} %copy-done.6) | copy-start | bytes 1572868
  141.2 40.5 %all-to-all-start.3 = ((bf16[64,72,128]{2,1,0:T(8,128)(2,1)}), bf16[64,72,128]{2,1,0:T(8,128)(2,1)S(1)}, u32[]{:S(2)}, u32[]{:S(2)}) async-start(bf16[64,72,128]{2,1,0:T(8,128)(2,1)} %filter_grad.1), calls=%async_computation.3 | async-start | bytes 2359296 | tf_op jit(solution)/shard_map/all_to_all | solution.py:502
  181.7 1.0 copy-start.1

commit v3 on v2

--- a/solution.py
+++ b/solution.py
@@ -138,18 +138,15 @@
     return lax.rsqrt(total(squares) / D + EPSILON)
 
 
-def mr_project_kernel(grad_signal, key_li, mixed, gain, *rest):
+def mr_project_kernel(ready, leave, grad_signal, key_li, mixed, gain, *rest):
     squares, grad_key_li, project = rest[:-2], rest[-2], rest[-1]
-    grad = grad_signal[...].astype(F32)
-    scaled = mixed[...].astype(F32) * inverse_rms(squares) * gain_block(gain, mixed.shape[0])
-    grad_scaled = grad * scaled
+    ready()
+    scaled = mixed[...].astype(F32) * inverse_rms(squares) * gain_column(gain[...])
+    grad_scaled = grad_signal[...].astype(F32) * scaled
+    project[...] = jnp.sum(grad_scaled * key_li[...].astype(F32), axis=0, keepdims=True)
+    leave[1]()
     grad_key_li[...] = grad_scaled.astype(BF16)
-
-    @pl.when(pl.program_id(0) == 0)
-    def _():
-        project[...] = jnp.zeros_like(project)
-
-    project[...] += jnp.sum(grad_scaled * key_li[...].astype(F32), axis=0, keepdims=True)
+    leave[0]()
 
 
 def against(spec, other):
@@ -204,10 +201,10 @@
 
 UNREAD = pl.BlockSpec(memory_space=pltpu.HBM)
 LIMIT = pltpu.CompilerParams(vmem_limit_bytes=60 * 1024 * 1024)
+STAGED_LIMIT = pltpu.CompilerParams(vmem_limit_bytes=28 * 1024 * 1024)
 PRODUCT_ROWS = 1024
 PAIR_ROWS = 1024
 FORWARD_ROWS = 1024
-PROJECT_ROWS = 1024
 BACKWARD_ROWS = 1024
 
 
@@ -235,6 +232,50 @@
 ROW = ((1, LANES), F32)
 
 
+def staged(kernel, name, here, fetched, unread, outs, scratch=()):
+    counts = [len(here), len(fetched), len(unread), len(outs), len(fetched), len(outs)]
+
+    def body(*refs):
+        groups, at = [], 0
+        for count in counts:
+            groups.append(refs[at : at + count])
+            at += count
+        near, far, _, far_outs, near_far, near_outs = groups
+        rest, arrived, left = refs[at:-2], refs[-2], refs[-1]
+        copies = [
+            pltpu.make_async_copy(source, target, arrived.at[i])
+            for i, (source, target) in enumerate(zip(far, near_far))
+        ]
+        for copy in copies:
+            copy.start()
+
+        def ready():
+            for copy in copies:
+                copy.wait()
+
+        backs = [
+            pltpu.make_async_copy(source, target, left.at[i])
+            for i, (source, target) in enumerate(zip(near_outs, far_outs))
+        ]
+        kernel(ready, [back.start for back in backs], *near, *near_far, *near_outs, *rest)
+        for back in backs:
+            back.wait()
+
+    return pl.pallas_call(
+        body,
+        in_specs=[pl.BlockSpec(memory_space=pltpu.VMEM)] * len(here)
+        + [UNREAD] * (len(fetched) + len(unread)),
+        out_specs=[UNREAD] * len(outs),
+        out_shape=[jax.ShapeDtypeStruct(*out) for out in outs],
+        scratch_shapes=[pltpu.VMEM(value.shape, value.dtype) for value in fetched]
+        + [pltpu.VMEM(*out) for out in outs]
+        + list(scratch)
+        + [pltpu.SemaphoreType.DMA((len(fetched),)), pltpu.SemaphoreType.DMA((len(outs),))],
+        compiler_params=STAGED_LIMIT,
+        name=name,
+    )(*here, *fetched, *unread)
+
+
 def product_of(key, value):
     rows = key.shape[0]
     each = row_spec(PRODUCT_ROWS)
@@ -268,14 +309,9 @@
 
 
 def mr_project(grad_signal, key_li, mixed, gain, squares):
-    rows = mixed.shape[0]
-    each = row_spec(PROJECT_ROWS)
-    return by_rows(
-        mr_project_kernel, "mr_project", PROJECT_ROWS, rows,
-        (grad_signal, key_li, mixed, gain, *squares),
-        [each] * 3 + [whole_spec(gain.shape)] + [whole_spec((1, LANES))] * len(squares),
-        [((rows, LANES), BF16), ROW],
-        [each, whole_spec((1, LANES))],
+    return staged(
+        mr_project_kernel, "mr_project", (grad_signal,), (key_li, mixed, gain, *squares), (),
+        [(mixed.shape, BF16), ROW],
     )
 
 
@@ -316,44 +352,29 @@
     )
 
 
-def deliver_kernel(bundled, gain, filter_grad, taps_grad, gain_grad):
+def deliver_kernel(ready, leave, bundled, gain, filter_grad, taps_grad, gain_grad):
     blocks = bundled.shape[0]
     width = filter_grad.shape[0] // blocks
-    values = bundled[...].astype(F32)
-    filter_grad[...] = values[:, :width, :].reshape(filter_grad.shape)
-    taps_grad[...] = values[:, width : 2 * width, :].reshape(taps_grad.shape)
+    filter_grad[...] = bundled[:, :width, :].astype(F32).reshape(filter_grad.shape)
+    leave[0]()
+    taps_grad[...] = bundled[:, width : 2 * width, :].astype(F32).reshape(taps_grad.shape)
+    leave[1]()
     together = LANES // width
-    step = pl.program_id(0)
     row = lax.broadcasted_iota(jnp.int32, (gain.shape[0], blocks), 0)
-    block = step * blocks + lax.broadcasted_iota(jnp.int32, (gain.shape[0], blocks), 1)
+    block = lax.broadcasted_iota(jnp.int32, (gain.shape[0], blocks), 1)
     own = jnp.where((block >= row * together) & (block < (row + 1) * together), 1.0, 0.0)
     own = own.astype(BF16)
-    high = values[:, 2 * width, :].astype(BF16)
-    low = values[:, 2 * width + 1, :].astype(BF16)
-
-    @pl.when(step == 0)
-    def _():
-        gain_grad[...] = jnp.zeros_like(gain_grad)
-
-    gain_grad[...] += dot(own, high) + dot(own, low)
-
-    @pl.when(step == pl.num_programs(0) - 1)
-    def _():
-        gain_grad[...] = gain_grad[...] / gain[...]
+    lines = bundled[:, 2 * width :, :].astype(F32)
+    high, low = lines[:, 0, :].astype(BF16), lines[:, 1, :].astype(BF16)
+    ready()
+    gain_grad[...] = (dot(own, high) + dot(own, low)) / gain[...]
+    leave[2]()
 
 
 def deliver(bundled, gain, blocks, width):
-    each = min(32, blocks)
-    rows = row_spec(each * width)
-    return by_rows(
-        deliver_kernel, "deliver", each, blocks,
-        (bundled, gain),
-        [
-            pl.BlockSpec((each,) + bundled.shape[1:], lambda i: (i, 0, 0)),
-            whole_spec(gain.shape),
-        ],
+    return staged(
+        deliver_kernel, "deliver", (bundled,), (gain,), (),
         [((blocks * width, LANES), F32)] * 2 + [(gain.shape, F32)],
-        [rows, rows, whole_spec(gain.shape)],
     )
 
 
@@ -403,10 +424,11 @@
 
 
 def signal_grad_kernel(
-    blocks, width, pair, unread, first, cosine, sine, second, second_back, last,
+    blocks, width, ready, leave, pair, first, cosine, sine, second, second_back, last,
     grad_out, cotan_spec, pair_flat, grad_flat,
 ):
     pair_flat[...] = pair[...].astype(F32)
+    ready()
 
     def one_group(step, carry):
         channels = [step * GROUP + at for at in range(GROUP)]
@@ -429,15 +451,18 @@
 
     lax.fori_loop(0, width // GROUP, one_group, 0)
     grad_out[...] = grad_flat[...].astype(BF16)
+    leave[0]()
+    leave[1]()
 
 
 def filter_grad_kernel(
-    blocks, width, together, moved, cotan_spec, grad_signal, unread, first, cosine, sine, second,
-    second_back, last, bundled, moved_flat, grad_flat,
+    blocks, width, together, ready, leave, moved, cotan_spec, grad_signal, first, cosine, sine,
+    second, second_back, last, bundled, moved_flat, grad_flat,
 ):
     moved_flat[...] = moved[...].reshape(moved_flat.shape).astype(F32)
     taps = jnp.sum(moved[:, :width, :].astype(F32), axis=0).astype(BF16)
     bundled[:, width : 2 * width, :] = jnp.broadcast_to(taps[None], (blocks, width, LANES))
+    ready()
     terms = moved[:, width:, :].astype(F32) * grad_signal[...].astype(F32)
     sums = jnp.sum(jnp.sum(terms, axis=0), axis=1, keepdims=True)
     high = sums.astype(BF16).astype(F32)
@@ -467,16 +492,15 @@
 
     lax.fori_loop(0, width // GROUP, one_group, 0)
     bundled[:, :width, :] = grad_flat[...].reshape(blocks, width, LANES).astype(BF16)
+    leave[0]()
 
 
 def signal_grad(pair, after, blocks, tables):
     rows = pair.shape[0] // 2
-    return by_rows(
-        functools.partial(signal_grad_kernel, blocks, rows // blocks), "signal_grad", 1, 1,
-        (pair, after, *tables),
-        [whole_spec(pair.shape), UNREAD] + [whole_spec(table.shape) for table in tables],
+    return staged(
+        functools.partial(signal_grad_kernel, blocks, rows // blocks), "signal_grad",
+        (pair,), tables, (after,),
         [((rows, LANES), BF16), ((rows, 2 * LANES), F32)],
-        [whole_spec((rows, LANES)), whole_spec((rows, 2 * LANES))],
         [pltpu.VMEM((2 * rows, LANES), F32), pltpu.VMEM((rows, LANES), F32)],
     )
 
@@ -484,16 +508,10 @@
 def filter_grad(moved, cotan_spec, grad_signal, after, tables):
     blocks, both, _ = moved.shape
     width = both // 2
-    ins = (moved, cotan_spec, grad_signal.reshape(blocks, width, LANES))
-    shape = (blocks, 2 * width + EXTRA, LANES)
-    return by_rows(
-        functools.partial(filter_grad_kernel, blocks, width, LANES // width), "filter_grad", 1, 1,
-        (*ins, after, *tables),
-        [whole_spec(value.shape) for value in ins]
-        + [UNREAD]
-        + [whole_spec(table.shape) for table in tables],
-        [(shape, BF16)],
-        [whole_spec(shape)],
+    return staged(
+        functools.partial(filter_grad_kernel, blocks, width, LANES // width), "filter_grad",
+        (moved,), (cotan_spec, grad_signal.reshape(blocks, width, LANES), *tables), (after,),
+        [((blocks, 2 * width + EXTRA, LANES), BF16)],
         [pltpu.VMEM((2 * blocks * width, LANES), F32), pltpu.VMEM((blocks * width, LANES), F32)],
     )[0]
 

time: 186 us -> 186 us (level)
  Pallas kernels: 37.4 us -> 33.4 us
  local copies, waits for them, and re-layouts: 4.47 us -> 7.33 us
    pallas_call x9 -> x5, Pallas kernels: 37.4 us -> 20.6 us  [by_rows(): pl.pallas_call(kernel, grid=(rows // count,), in_specs=in_specs, out_spec...]
    pallas_call x0 -> x4, Pallas kernels: none -> 12.9 us  [staged(): pl.pallas_call(body, in_specs=[pl.BlockSpec(memory_space=pltpu.VMEM)] * l...]
    unnamed x30 -> x54, local copies, waits for them, and re-layouts: 4.47 us -> 7.33 us
  transfers between devices with their start and end apart: 12 -> 12, of which waited for: 9 -> 8; matrix products, arithmetic and copies ran while one was open for 1% -> 1% of each run, Pallas kernels for 7% -> 7%
where the time goes in v3:
time: 186 us; the launch traced here: 185 us
  waiting for transfers between devices  83.8 us (45%)
  starting transfers between devices  56.7 us (30%)
  Pallas kernels  33.4 us (18%)
  local copies, waits for them, and re-layouts  7.33 us (4%)
  other arithmetic  2.46 us (1%)
    ppermute x2, waiting for transfers between devices, shifted(): return lax.ppermute(block, 'ctx', route)  46.4 us
    all_to_all x4, starting transfers between devices, swapped(): return lax.all_to_all(rows, 'ctx', split_axis=0, concat_axis=0, tiled=True)  43.1 us
    all_to_all x4, waiting for transfers between devices, swapped(): return lax.all_to_all(rows, 'ctx', split_axis=0, concat_axis=0, tiled=True)  31.1 us
    pallas_call x5, Pallas kernels, by_rows(): pl.pallas_call(kernel, grid=(rows // count,), in_specs=in_specs, out_spec...  20.6 us
    pallas_call x4, Pallas kernels, staged(): pl.pallas_call(body, in_specs=[pl.BlockSpec(memory_space=pltpu.VMEM)] * l...  12.9 us
    ppermute x6, starting transfers between devices, parts_over_ch(): return [row] + [lax.ppermute(row, 'ch', route) for route in routes]  7.69 us
    unnamed x54, local copies, waits for them, and re-layouts  7.33 us
    ppermute x6, waiting for transfers between devices, parts_over_ch(): return [row] + [lax.ppermute(row, 'ch', route) for route in routes]  6.25 us
  transfers between devices with their start and end apart: 12, of which 8 were waited for; matrix products, arithmetic and copies ran while one was open for 1% of the time, Pallas kernels for 7%

profile of v3, /device:TPU:1, one launch (start us, length us, event | category | flops | bytes accessed | tf_op | source)
XLA Modules:
  0.0 184.8 jit_solution(14758876129715410026)
XLA Ops:
  0.6 2.2 %pair_up.1 = bf16[64,64,128]{2,1,0:T(8,128)(2,1)} custom-call(bf16[2048,128]{1,0:T(8,128)(2,1)} %cotan.1, f32[2048,128]{1,0:T(8,128)} %filt.1), custom_call_target="tpu_custom_call" | custom-call | tf_op jit(solution)/shard_map/pair_up/pallas_call | solution.py:220
  2.9 13.1 %all-to-all-start = ((bf16[64,64,128]{2,1,0:T(8,128)(2,1)}), bf16[64,64,128]{2,1,0:T(8,128)(2,1)S(1)}, u32[]{:S(2)}, u32[]{:S(2)}) async-start(bf16[64,64,128]{2,1,0:T(8,128)(2,1)} %pair_up.1), calls=%async_computation | async-start | bytes 2097152 | tf_op jit(solution)/shard_map/all_to_all | solution.py:520
  16.0 2.0 %product_of.1 = bf16[2048,128]{1,0:T(8,128)(2,1)} custom-call(bf16[2048,128]{1,0:T(8,128)(2,1)} %key.3, bf16[2048,128]{1,0:T(8,128)(2,1)} %value.3), custom_call_target="tpu_custom_call" | custom-call | tf_op jit(solution)/shard_map/product_of/pallas_call | solution.py:220
  18.0 3.5 %collective-permute-start = (bf16[2048,128]{1,0:T(8,128)(2,1)}, bf16[2048,128]{1,0:T(8,128)(2,1)S(1)}, u32[]{:S(2)}, u32[]{:S(2)}) collective-permute-start(bf16[2048,128]{1,0:T(8,128)(2,1)} %product_of.1), channel_id=1, source_target_pairs={{0,4},{4,8},{8,12},{12,16},{16,20},{20,24},{24,28},{28,32},{32,36}... | collective-permute-start | bytes 1572872 | tf_op jit(solution)/shard_map/ppermute | solution.py:532
  21.5 23.0 %collective-permute-done.refs_7_.prior = bf16[2048,128]{1,0:T(8,128)(2,1)S(1)} collective-permute-done((bf16[2048,128]{1,0:T(8,128)(2,1)}, bf16[2048,128]{1,0:T(8,128)(2,1)S(1)}, u32[]{:S(2)}, u32[]{:S(2)}) %collective-permute-start) | collective-permute-done | bytes 524320 | tf_op jit(solution)/shard_map/ppermute | solution.py:532
  44.6 0.8 copy-done.6
  45.4 1.0 copy-done.7
  46.5 4.9 %signal_grad.1 = (bf16[2048,128]{1,0:T(8,128)(2,1)}, f32[2048,256]{1,0:T(8,128)S(1)}) custom-call(bf16[4096,128]{1,0:T(8,128)(2,1)S(1)} %bitcast.8, bf16[128,128]{1,0:T(8,128)(2,1)S(1)} %copy-done.11, f32[64,128]{1,0:T(8,128)S(1)} %copy-done.13, f32[64,128]{1,0:T(8,128)S(1)} %copy-done.12, bf16[256,256]{1,0:T(8,128)(2,1)S(1)} %copy-done.9, ...), custom_call_target="tpu_custom_call" | custom-call | tf_op jit(solution)/shard_map/signal_grad/pallas_call | solution.py:264
  51.3 11.3 %all-to-all-start.1 = ((bf16[64,32,128]{2,1,0:T(8,128)(2,1)}), bf16[64,32,128]{2,1,0:T(8,128)(2,1)S(1)}, u32[]{:S(2)}, u32[]{:S(2)}) async-start(bf16[64,32,128]{2,1,0:T(8,128)(2,1)} %bitcast.1.refs_2_), calls=%async_computation.1 | async-start | bytes 1048576 | tf_op jit(solution)/shard_map/all_to_all | solution.py:520
  62.6 7.3 %mr_forward.1 = (f32[2048,128]{1,0:T(8,128)}, bf16[2048,128]{1,0:T(8,128)(2,1)}, f32[2048,256]{1,0:T(8,128)}, f32[2048,256]{1,0:T(8,128)}, f32[1,128]{1,0:T(1,128)}) custom-call(bf16[2048,128]{1,0:T(8,128)(2,1)} %key.3, bf16[2048,128]{1,0:T(8,128)(2,1)} %value.3, bf16[2048,128]{1,0:T(8,128)(2,1)} %copy-done.6, bf16[2048,128]{1,0:T(8,128)(2,1)} %query.3, ...), custom_call_target="tpu_custom_call" | custom-call | tf_op jit(solution)/shard_map/mr_forward/pallas_call | solution.py:220
  70.0 2.8 %collective-permute-start.3 = (f32[1,128]{1,0:T(1,128)}, f32[1,128]{1,0:T(1,128)S(1)}, u32[]{:S(2)}, u32[]{:S(2)}) collective-permute-start(f32[1,128]{1,0:T(1,128)} %get-tuple-element.28.refs_4_.rest_4_), channel_id=1, source_target_pairs={{0,3},{1,0},{2,1},{3,2},{4,7},{5,4},{6,5},{7,6},{8,11},{9,8},{10,9... | collective-permute-start | bytes 1544 | tf_op jit(solution)/shard_map/ppermute | solution.py:526
  73.1 0.7 collective-permute-start.1
  73.8 3.3 %collective-permute-done.2.refs_6_.rest_6_ = f32[1,128]{1,0:T(1,128)S(1)} collective-permute-done((f32[1,128]{1,0:T(1,128)}, f32[1,128]{1,0:T(1,128)S(1)}, u32[]{:S(2)}, u32[]{:S(2)}) %collective-permute-start.2) | collective-permute-done | bytes 544 | tf_op jit(solution)/shard_map/ppermute | solution.py:526
  77.7 2.2 %all-to-all-done.1 = bf16[64,32,128]{2,1,0:T(8,128)(2,1)S(1)} async-done(((bf16[64,32,128]{2,1,0:T(8,128)(2,1)}), bf16[64,32,128]{2,1,0:T(8,128)(2,1)S(1)}, u32[]{:S(2)}, u32[]{:S(2)}) %all-to-all-start.1) | async-done | bytes 524320 | tf_op jit(solution)/shard_map/all_to_all | solution.py:520
  80.0 1.2 copy-done.2
  81.2 0.7 copy-done.16
  82.5 1.7 mr_project.1
  84.2 2.8 %collective-permute-start.6 = (f32[1,128]{1,0:T(1,128)S(1)}, f32[1,128]{1,0:T(1,128)S(1)}, u32[]{:S(2)}, u32[]{:S(2)}) collective-permute-start(f32[1,128]{1,0:T(1,128)S(1)} %get-tuple-element.29.rest_0_), channel_id=1, source_target_pairs={{0,3},{1,0},{2,1},{3,2},{4,7},{5,4},{6,5},{7,6},{8,11},{9,8},{10,9... | collective-permute-start | bytes 1544 | tf_op jit(solution)/shard_map/ppermute | solution.py:526
  87.3 0.7 collective-permute-start.4
  88.0 2.8 %collective-permute-done.5.rest_2_ = f32[1,128]{1,0:T(1,128)S(1)} collective-permute-done((f32[1,128]{1,0:T(1,128)S(1)}, f32[1,128]{1,0:T(1,128)S(1)}, u32[]{:S(2)}, u32[]{:S(2)}) %collective-permute-start.5) | collective-permute-done | bytes 544 | tf_op jit(solution)/shard_map/ppermute | solution.py:526
  91.5 4.5 %taps_grad_of.1 = (bf16[64,64,128]{2,1,0:T(8,128)(2,1)}, f32[2048,256]{1,0:T(8,128)}) custom-call(bf16[2048,128]{1,0:T(8,128)(2,1)} %bitcast.6, bf16[2048,128]{1,0:T(8,128)(2,1)} %key_li.3, bf16[2048,128]{1,0:T(8,128)(2,1)} %get-tuple-element.25.refs_2_.mixed, bf16[2048,128]{1,0:T(8,128)(2,1)} %query.3, f32[16,128]{1,0:T(8,128)} %bitcast.9, ...), custom_call_target="tpu_custom_call" | custom-call | tf_op jit(solution)/shard_map/taps_grad_of/pallas_call | solution.py:220
  96.0 9.6 %all-to-all-start.2 = ((bf16[64,64,128]{2,1,0:T(8,128)(2,1)}), bf16[64,64,128]{2,1,0:T(8,128)(2,1)S(1)}, u32[]{:S(2)}, u32[]{:S(2)}) async-start(bf16[64,64,128]{2,1,0:T(8,128)(2,1)} %get-tuple-element.36), calls=%async_computation.2 | async-start | bytes 2097152 | tf_op jit(solution)/shard_map/all_to_all | solution.py:520
  105.6 4.5 %product_grad_of.1 = (bf16[2048,128]{1,0:T(8,128)(2,1)}, bf16[2048,128]{1,0:T(8,128)(2,1)}, f32[2048,128]{1,0:T(8,128)}) custom-call(bf16[2048,128]{1,0:T(8,128)(2,1)} %bitcast.7, bf16[2048,128]{1,0:T(8,128)(2,1)} %key_li.3, bf16[2048,128]{1,0:T(8,128)(2,1)} %get-tuple-element.25.refs_2_.mixed, f32[2048,128]{1,0:T(8,128)} %get-tuple-element.26.conv, ...), custom_call_target="tpu_custom_call" | custom-call | tf_op jit(solution)/shard_map/product_grad_of/pallas_call | solution.py:220
  110.1 2.4 %collective-permute-start.7 = (bf16[2048,128]{1,0:T(8,128)(2,1)}, bf16[2048,128]{1,0:T(8,128)(2,1)S(1)}, u32[]{:S(2)}, u32[]{:S(2)}) collective-permute-start(bf16[2048,128]{1,0:T(8,128)(2,1)} %get-tuple-element.34), channel_id=1, source_target_pairs={{4,0},{8,4},{12,8},{16,12},{20,16},{24,20},{28,24},{32,28},{36,32}... | collective-permute-start | bytes 1572872 | tf_op jit(solution)/shard_map/ppermute | solution.py:532
  112.5 23.4 %collective-permute-done.7.refs_9_ = bf16[2048,128]{1,0:T(8,128)(2,1)S(1)} collective-permute-done((bf16[2048,128]{1,0:T(8,128)(2,1)}, bf16[2048,128]{1,0:T(8,128)(2,1)S(1)}, u32[]{:S(2)}, u32[]{:S(2)}) %collective-permute-start.7) | collective-permute-done | bytes 524320 | tf_op jit(solution)/shard_map/ppermute | solution.py:532
  135.9 0.8 copy-done.3
  136.7 1.0 copy-done.4
  137.7 4.9 %filter_grad.1 = bf16[64,72,128]{2,1,0:T(8,128)(2,1)} custom-call(bf16[64,64,128]{2,1,0:T(8,128)(2,1)S(1)} %all-to-all-done.2.refs_0_, f32[2048,256]{1,0:T(8,128)S(1)} %get-tuple-element.37.refs_1_, bf16[64,32,128]{2,1,0:T(8,128)(2,1)} %bitcast.1.refs_2_, bf16[128,128]{1,0:T(8,128)(2,1)S(1)} %copy-done.11, f32[64,128]{1,0:T(8,128)S(1)} %copy-done.13, ...), custom_call_target="tpu_custom_call" | custom-call | tf_op jit(solution)/shard_map/filter_grad/pallas_call | solution.py:264
  142.7 9.1 %all-to-all-start.3 = ((bf16[64,72,128]{2,1,0:T(8,128)(2,1)}), bf16[64,72,128]{2,1,0:T(8,128)(2,1)S(1)}, u32[]{:S(2)}, u32[]{:S(2)}) async-start(bf16[64,72,128]{2,1,0:T(8,128)(2,1)} %filter_grad.1), calls=%async_computation.3 | async-start | bytes 2359296 | tf_op jit(solution)/shard_map/all_to_all | solution.py:520
  151.9 2.5 %multiply_convert_fusion = (bf16[2048,128]{1,0:T(8,128)(2,1)}, bf16[2048,128]{1,0:T(8,128)(2,1)}) fusion(bf16[2048,128]{1,0:T(8,128)(2,1)S(1)} %copy-done.22, f32[2048,128]{1,0:T(8,128)} %get-tuple-element.33, bf16[2048,128]{1,0:T(8,128)(2,1)S(1)} %copy-done.5, bf16[2048,128]{1,0:T(8,128)(2,1)S(1)} %copy-done.23), kind=kLoop, calls=%fused_computation | loop fusion | flops 2097152 | bytes 3670016 | tf_op jit(solution)/shard_map/convert_element_type | solution.py:562
  154.3 28.9 %all-to-all-done.3.refs_0_ = bf16[64,72,128]{2,1,0:T(8,128)(2,1)S(1)} async-done(((bf16[64,72,128]{2,1,0:T(8,128)(2,1)}), bf16[64,72,128]{2,1,0:T(8,128)(2,1)S(1)}, u32[]{:S(2)}, u32[]{:S(2)}) %all-to-all-start.3) | async-done | bytes 1179680 | tf_op jit(solution)/shard_map/all_to_all | solution.py:520
  183.2 1.4 deliver.1
  (56 shorter events, 2.6 us)
Async XLA Ops:
  2.8 42.5 %copy-start.8 = (bf16[256,256]{1,0:T(8,128)(2,1)S(1)}, bf16[256,256]{1,0:T(8,128)(2,1)}, u32[]{:S(2)}) copy-start(bf16[256,256]{1,0:T(8,128)(2,1)} %constant.35.clone.refs_5_.refs_7_) | copy-start | bytes 393220
  2.9 42.5 %copy-start.9 = (bf16[256,256]{1,0:T(8,128)(2,1)S(1)}, bf16[256,256]{1,0:T(8,128)(2,1)}, u32[]{:S(2)}) copy-start(bf16[256,256]{1,0:T(8,128)(2,1)} %constant.34.clone.refs_4_.refs_6_) | copy-start | bytes 393220
  2.9 42.5 %copy-start.10 = (bf16[64,256]{1,0:T(8,128)(2,1)S(1)}, bf16[64,256]{1,0:T(8,128)(2,1)}, u32[]{:S(2)}) copy-start(bf16[64,256]{1,0:T(8,128)(2,1)} %constant.37.refs_6_.refs_8_) | copy-start | bytes 98308
  2.9 42.5 %copy-start.11 = (bf16[128,128]{1,0:T(8,128)(2,1)S(1)}, bf16[128,128]{1,0:T(8,128)(2,1)}, u32[]{:S(2)}) copy-start(bf16[128,128]{1,0:T(8,128)(2,1)} %constant.36.refs_1_.refs_3_) | copy-start | bytes 98308
  2.9 42.5 %copy-start.12 = (f32[64,128]{1,0:T(8,128)S(1)}, f32[64,128]{1,0:T(8,128)}, u32[]{:S(2)}) copy-start(f32[64,128]{1,0:T(8,128)} %constant.33.clone.refs_3_.refs_5_) | copy-start | bytes 98308
  2.9 42.5 %copy-start.13 = (f32[64,128]{1,0:T(8,128)S(1)}, f32[64,128]{1,0:T(8,128)}, u32[]{:S(2)}) copy-start(f32[64,128]{1,0:T(8,128)} %constant.32.clone.refs_2_.refs_4_) | copy-start | bytes 98308
  2.9 42.5 %all-to-all-start = ((bf16[64,64,128]{2,1,0:T(8,128)(2,1)}), bf16[64,64,128]{2,1,0:T(8,128)(2,1)S(1)}, u32[]{:S(2)}, u32[]{:S(2)}) async-start(bf16[64,64,128]{2,1,0:T(8,128)(2,1)} %pair_up.1), calls=%async_computation | async-start | bytes 2097152 | tf_op jit(solution)/shard_map/all_to_all | solution.py:520
  18.0 26.6 %collective-permute-start = (bf16[2048,128]{1,0:T(8,128)(2,1)}, bf16[2048,128]{1,0:T(8,128)(2,1)S(1)}, u32[]{:S(2)}, u32[]{:S(2)}) collective-permute-start(bf16[2048,128]{1,0:T(8,128)(2,1)} %product_of.1), channel_id=1, source_target_pairs={{0,4},{4,8},{8,12},{12,16},{16,20},{20,24},{24,28},{28,32},{32,36}... | collective-permute-start | bytes 1572872 | tf_op jit(solution)/shard_map/ppermute | solution.py:532
  45.4 1.0 copy-start.7
  51.3 28.6 %all-to-all-start.1 = ((bf16[64,32,128]{2,1,0:T(8,128)(2,1)}), bf16[64,32,128]{2,1,0:T(8,128)(2,1)S(1)}, u32[]{:S(2)}, u32[]{:S(2)}) async-start(bf16[64,32,128]{2,1,0:T(8,128)(2,1)} %bitcast.1.refs_2_), calls=%async_computation.1 | async-start | bytes 1048576 | tf_op jit(solution)/shard_map/all_to_all | solution.py:520
  62.6 17.3 %copy-start.1 = (bf16[2048,128]{1,0:T(8,128)(2,1)S(1)}, bf16[2048,128]{1,0:T(8,128)(2,1)}, u32[]{:S(2)}) copy-start(bf16[2048,128]{1,0:T(8,128)(2,1)} %key_li.3) | copy-start | bytes 1572868
  62.6 17.3 %copy-start.14 = (f32[2048]{0:T(1024)S(1)}, f32[2048]{0:T(1024)}, u32[]{:S(2)}) copy-start(f32[2048]{0:T(1024)} %param.25) | copy-start | bytes 24580
  70.0 3.8 %collective-permute-start.3 = (f32[1,128]{1,0:T(1,128)}, f32[1,128]{1,0:T(1,128)S(1)}, u32[]{:S(2)}, u32[]{:S(2)}) collective-permute-start(f32[1,128]{1,0:T(1,128)} %get-tuple-element.28.refs_4_.rest_4_), channel_id=1, source_target_pairs={{0,3},{1,0},{2,1},{3,2},{4,7},{5,4},{6,5},{7,6},{8,11},{9,8},{10,9... | collective-permute-start | bytes 1544 | tf_op jit(solution)/shard_map/ppermute | solution.py:526
  72.8 4.3 %collective-permute-start.2 = (f32[1,128]{1,0:T(1,128)}, f32[1,128]{1,0:T(1,128)S(1)}, u32[]{:S(2)}, u32[]{:S(2)}) collective-permute-start(f32[1,128]{1,0:T(1,128)} %get-tuple-element.28.refs_4_.rest_4_), channel_id=1, source_target_pairs={{0,2},{1,3},{2,0},{3,1},{4,6},{5,7},{6,4},{7,5},{8,10},{9,11},{10,... | collective-permute-start | bytes 1544 | tf_op jit(solution)/shard_map/ppermute | solution.py:526
  73.1 4.0 %collective-permute-start.1 = (f32[1,128]{1,0:T(1,128)}, f32[1,128]{1,0:T(1,128)S(1)}, u32[]{:S(2)}, u32[]{:S(2)}) collective-permute-start(f32[1,128]{1,0:T(1,128)} %get-tuple-element.28.refs_4_.rest_4_), channel_id=1, source_target_pairs={{0,1},{1,2},{2,3},{3,0},{4,5},{5,6},{6,7},{7,4},{8,9},{9,10},{10,1... | collective-permute-start | bytes 1544 | tf_op jit(solution)/shard_map/ppermute | solution.py:526
  73.8 17.1 %copy-start.17 = (f32[1,128]{1,0:T(1,128)}, f32[1,128]{1,0:T(1,128)S(1)}, u32[]{:S(2)}) copy-start(f32[1,128]{1,0:T(1,128)S(1)} %collective-permute-done.3.refs_7_.rest_7_) | copy-start | bytes 1540
  77.1 13.8 %copy-start.18 = (f32[1,128]{1,0:T(1,128)}, f32[1,128]{1,0:T(1,128)S(1)}, u32[]{:S(2)}) copy-start(f32[1,128]{1,0:T(1,128)S(1)} %collective-permute-done.2.refs_6_.rest_6_) | copy-start | bytes 1540
  79.9 11.0 %copy-start = (bf16[64,32,128]{2,1,0:T(8,128)(2,1)}, bf16[64,32,128]{2,1,0:T(8,128)(2,1)S(1)}, u32[]{:S(2)}) copy-start(bf16[64,32,128]{2,1,0:T(8,128)(2,1)S(1)} %all-to-all-done.1) | copy-start | bytes 1572868
  80.0 1.2 copy-start.2
  84.2 6.8 %copy-start.21 = (f32[1,128]{1,0:T(1,128)}, f32[1,128]{1,0:T(1,128)S(1)}, u32[]{:S(2)}) copy-start(f32[1,128]{1,0:T(1,128)S(1)} %get-tuple-element.29.rest_0_) | copy-start | bytes 1540
  84.2 3.9 %collective-permute-start.6 = (f32[1,128]{1,0:T(1,128)S(1)}, f32[1,128]{1,0:T(1,128)S(1)}, u32[]{:S(2)}, u32[]{:S(2)}) collective-permute-start(f32[1,128]{1,0:T(1,128)S(1)} %get-tuple-element.29.rest_0_), channel_id=1, source_target_pairs={{0,3},{1,0},{2,1},{3,2},{4,7},{5,4},{6,5},{7,6},{8,11},{9,8},{10,9... | collective-permute-start | bytes 1544 | tf_op jit(solution)/shard_map/ppermute | solution.py:526
  87.0 3.9 %collective-permute-start.5 = (f32[1,128]{1,0:T(1,128)S(1)}, f32[1,128]{1,0:T(1,128)S(1)}, u32[]{:S(2)}, u32[]{:S(2)}) collective-permute-start(f32[1,128]{1,0:T(1,128)S(1)} %get-tuple-element.29.rest_0_), channel_id=1, source_target_pairs={{0,2},{1,3},{2,0},{3,1},{4,6},{5,7},{6,4},{7,5},{8,10},{9,11},{10,... | collective-permute-start | bytes 1544 | tf_op jit(solution)/shard_map/ppermute | solution.py:526
  87.3 3.6 %collective-permute-start.4 = (f32[1,128]{1,0:T(1,128)S(1)}, f32[1,128]{1,0:T(1,128)S(1)}, u32[]{:S(2)}, u32[]{:S(2)}) collective-permute-start(f32[1,128]{1,0:T(1,128)S(1)} %get-tuple-element.29.rest_0_), channel_id=1, source_target_pairs={{0,1},{1,2},{2,3},{3,0},{4,5},{5,6},{6,7},{7,4},{8,9},{9,10},{10,1... | collective-permute-start | bytes 1544 | tf_op jit(solution)/shard_map/ppermute | solution.py:526
  88.0 2.9 %copy-start.24 = (f32[1,128]{1,0:T(1,128)}, f32[1,128]{1,0:T(1,128)S(1)}, u32[]{:S(2)}) copy-start(f32[1,128]{1,0:T(1,128)S(1)} %collective-permute-done.6.rest_3_) | copy-start | bytes 1540
  96.0 40.7 %all-to-all-start.2 = ((bf16[64,64,128]{2,1,0:T(8,128)(2,1)}), bf16[64,64,128]{2,1,0:T(8,128)(2,1)S(1)}, u32[]{:S(2)}, u32[]{:S(2)}) async-start(bf16[64,64,128]{2,1,0:T(8,128)(2,1)} %get-tuple-element.36), calls=%async_computation.2 | async-start | bytes 2097152 | tf_op jit(solution)/shard_map/all_to_all | solution.py:520
  110.1 25.7 %collective-permute-start.7 = (bf16[2048,128]{1,0:T(8,128)(2,1)}, bf16[2048,128]{1,0:T(8,128)(2,1)S(1)}, u32[]{:S(2)}, u32[]{:S(2)}) collective-permute-start(bf16[2048,128]{1,0:T(8,128)(2,1)} %get-tuple-element.34), channel_id=1, source_target_pairs={{4,0},{8,4},{12,8},{16,12},{20,16},{24,20},{28,24},{32,28},{36,32}... | collective-permute-start | bytes 1572872 | tf_op jit(solution)/shard_map/ppermute | solution.py:532
  136.7 1.0 copy-start.4
  142.6 9.2 %copy-start.5 = (bf16[2048,128]{1,0:T(8,128)(2,1)S(1)}, bf16[2048,128]{1,0:T(8,128)(2,1)}, u32[]{:S(2)}) copy-start(bf16[2048,128]{1,0:T(8,128)(2,1)} %copy-done.3) | copy-start | bytes 1572868
  142.6 9.2 %copy-start.22 = (bf16[2048,128]{1,0:T(8,128)(2,1)S(1)}, bf16[2048,128]{1,0:T(8,128)(2,1)}, u32[]{:S(2)}) copy-start(bf16[2048,128]{1,0:T(8,128)(2,1)} %key.3) | copy-start | bytes 1572868
  142.7 9.2 %copy-start.23 = (bf16[2048,128]{1,0:T(8,128)(2,1)S(1)}, bf16[2048,128]{1,0:T(8,128)(2,1)}, u32[]{:S(2)}) copy-start(bf16[2048,128]{1,0:T(8,128)(2,1)} %value.3) | copy-start | bytes 1572868
  142.7 40.5 %all-to-all-start.3 = ((bf16[64,72,128]{2,1,0:T(8,128)(2,1)}), bf16[64,72,128]{2,1,0:T(8,128)(2,1)S(1)}, u32[]{:S(2)}, u32[]{:S(2)}) async-start(bf16[64,72,128]{2,1,0:T(8,128)(2,1)} %filter_grad.1), calls=%async_computation.3 | async-start | bytes 2359296 | tf_op jit(solution)/shard_map/all_to_all | solution.py:520
  151.8 31.4 %copy-start.15 = (f32[2048]{0:T(1024)S(1)}, f32[2048]{0:T(1024)}, u32[]{:S(2)}) copy-start(f32[2048]{0:T(1024)} %param.25) | copy-start | bytes 24580
  (7 other events, 4.5 us)

commit v4 on v3

--- a/solution.py
+++ b/solution.py
@@ -541,7 +541,7 @@
     gain = norm_gain.reshape(-1, LANES)
     moved_pair = swapped(pair_up(cotangent, filter_li, blocks)).reshape(2 * rows, LANES)
     prior = shifted(product_of(key_mr, value_mr), 1)
-    grad_moved, cotan_spec = signal_grad(moved_pair, prior, blocks, long)
+    grad_moved, cotan_spec = signal_grad(moved_pair, prior[:16], blocks, long)
     grad_signal = swapped(grad_moved)
     conv, mixed, window_spec, taps_spec, squares = mr_forward(
         key_mr, value_mr, prior, query_mr, filter_mr, grad_moved, short
@@ -560,7 +560,7 @@
     grad_product = own_grad + after.astype(F32)
     grad_key = (grad_product * value_mr.astype(F32)).astype(BF16)
     grad_value = (grad_product * key_mr.astype(F32)).astype(BF16)
-    bundled = filter_grad(moved, cotan_spec, grad_moved, after, long)
+    bundled = filter_grad(moved, cotan_spec, grad_moved, after[:16], long)
     grad_filter_li, grad_filter_mr, gain_rows = deliver(swapped(bundled), gain, blocks, width)
     grad_gain = gain_rows.reshape(rows)
     return (

time: 186 us -> 183 us (0.984)
  local copies, waits for them, and re-layouts: 7.33 us -> 5.1 us
    unnamed x54 -> x50, local copies, waits for them, and re-layouts: 7.33 us -> 5.1 us
  transfers between devices with their start and end apart: 12 -> 12, of which waited for: 8 -> 9; matrix products, arithmetic and copies ran while one was open for 1% -> 1% of each run, Pallas kernels for 7% -> 8%
where the time goes in v4:
time: 183 us
  waiting for transfers between devices  84.1 us (46%)
  starting transfers between devices  56.8 us (31%)
  Pallas kernels  33.5 us (18%)
  local copies, waits for them, and re-layouts  5.1 us (3%)
  other arithmetic  2.28 us (1%)
    ppermute x2, waiting for transfers between devices, shifted(): return lax.ppermute(block, 'ctx', route)  46.4 us
    all_to_all x4, starting transfers between devices, swapped(): return lax.all_to_all(rows, 'ctx', split_axis=0, concat_axis=0, tiled=True)  43.2 us
    all_to_all x4, waiting for transfers between devices, swapped(): return lax.all_to_all(rows, 'ctx', split_axis=0, concat_axis=0, tiled=True)  31.4 us
    pallas_call x5, Pallas kernels, by_rows(): pl.pallas_call(kernel, grid=(rows // count,), in_specs=in_specs, out_spec...  20.6 us
    pallas_call x4, Pallas kernels, staged(): pl.pallas_call(body, in_specs=[pl.BlockSpec(memory_space=pltpu.VMEM)] * l...  12.9 us
    ppermute x6, starting transfers between devices, parts_over_ch(): return [row] + [lax.ppermute(row, 'ch', route) for route in routes]  7.7 us
    ppermute x6, waiting for transfers between devices, parts_over_ch(): return [row] + [lax.ppermute(row, 'ch', route) for route in routes]  6.24 us
    ppermute x2, starting transfers between devices, shifted(): return lax.ppermute(block, 'ctx', route)  5.89 us
  transfers between devices with their start and end apart: 12, of which 9 were waited for; matrix products, arithmetic and copies ran while one was open for 1% of the time, Pallas kernels for 8%

profile of v4, /device:TPU:1, one launch (start us, length us, event | category | flops | bytes accessed | tf_op | source)
XLA Modules:
  0.0 182.7 jit_solution(7403262826529838830)
XLA Ops:
  0.6 2.2 %pair_up.1 = bf16[64,64,128]{2,1,0:T(8,128)(2,1)} custom-call(bf16[2048,128]{1,0:T(8,128)(2,1)} %cotan.1, f32[2048,128]{1,0:T(8,128)} %filt.1), custom_call_target="tpu_custom_call" | custom-call | tf_op jit(solution)/shard_map/pair_up/pallas_call | solution.py:220
  2.9 13.1 %all-to-all-start = ((bf16[64,64,128]{2,1,0:T(8,128)(2,1)}), bf16[64,64,128]{2,1,0:T(8,128)(2,1)S(1)}, u32[]{:S(2)}, u32[]{:S(2)}) async-start(bf16[64,64,128]{2,1,0:T(8,128)(2,1)} %pair_up.1), calls=%async_computation | async-start | bytes 2097152 | tf_op jit(solution)/shard_map/all_to_all | solution.py:520
  16.0 2.0 %product_of.1 = bf16[2048,128]{1,0:T(8,128)(2,1)} custom-call(bf16[2048,128]{1,0:T(8,128)(2,1)} %key.3, bf16[2048,128]{1,0:T(8,128)(2,1)} %value.3), custom_call_target="tpu_custom_call" | custom-call | tf_op jit(solution)/shard_map/product_of/pallas_call | solution.py:220
  18.0 3.5 %collective-permute-start = (bf16[2048,128]{1,0:T(8,128)(2,1)}, bf16[2048,128]{1,0:T(8,128)(2,1)S(1)}, u32[]{:S(2)}, u32[]{:S(2)}) collective-permute-start(bf16[2048,128]{1,0:T(8,128)(2,1)} %product_of.1), channel_id=1, source_target_pairs={{0,4},{4,8},{8,12},{12,16},{16,20},{20,24},{24,28},{28,32},{32,36}... | collective-permute-start | bytes 1572872 | tf_op jit(solution)/shard_map/ppermute | solution.py:532
  21.5 23.0 %collective-permute-done.prior = bf16[2048,128]{1,0:T(8,128)(2,1)S(1)} collective-permute-done((bf16[2048,128]{1,0:T(8,128)(2,1)}, bf16[2048,128]{1,0:T(8,128)(2,1)S(1)}, u32[]{:S(2)}, u32[]{:S(2)}) %collective-permute-start) | collective-permute-done | bytes 524320 | tf_op jit(solution)/shard_map/ppermute | solution.py:532
  44.8 0.6 copy-done.21
  45.4 4.9 %signal_grad.1 = (bf16[2048,128]{1,0:T(8,128)(2,1)}, f32[2048,256]{1,0:T(8,128)S(1)}) custom-call(bf16[4096,128]{1,0:T(8,128)(2,1)S(1)} %bitcast.8, bf16[128,128]{1,0:T(8,128)(2,1)S(1)} %copy-done.8, f32[64,128]{1,0:T(8,128)S(1)} %copy-done.10, f32[64,128]{1,0:T(8,128)S(1)} %copy-done.9, bf16[256,256]{1,0:T(8,128)(2,1)S(1)} %copy-done.4, ...), custom_call_target="tpu_custom_call" | custom-call | tf_op jit(solution)/shard_map/signal_grad/pallas_call | solution.py:264
  50.3 11.3 %all-to-all-start.1 = ((bf16[64,32,128]{2,1,0:T(8,128)(2,1)}), bf16[64,32,128]{2,1,0:T(8,128)(2,1)S(1)}, u32[]{:S(2)}, u32[]{:S(2)}) async-start(bf16[64,32,128]{2,1,0:T(8,128)(2,1)} %bitcast.1.refs_2_), calls=%async_computation.1 | async-start | bytes 1048576 | tf_op jit(solution)/shard_map/all_to_all | solution.py:520
  61.6 7.3 %mr_forward.1 = (f32[2048,128]{1,0:T(8,128)}, bf16[2048,128]{1,0:T(8,128)(2,1)}, f32[2048,256]{1,0:T(8,128)}, f32[2048,256]{1,0:T(8,128)}, f32[1,128]{1,0:T(1,128)}) custom-call(bf16[2048,128]{1,0:T(8,128)(2,1)} %key.3, bf16[2048,128]{1,0:T(8,128)(2,1)} %value.3, bf16[2048,128]{1,0:T(8,128)(2,1)} %copy-done.21, bf16[2048,128]{1,0:T(8,128)(2,1)} %query.3, ...), custom_call_target="tpu_custom_call" | custom-call | tf_op jit(solution)/shard_map/mr_forward/pallas_call | solution.py:220
  69.0 2.8 %collective-permute-start.3 = (f32[1,128]{1,0:T(1,128)}, f32[1,128]{1,0:T(1,128)S(1)}, u32[]{:S(2)}, u32[]{:S(2)}) collective-permute-start(f32[1,128]{1,0:T(1,128)} %get-tuple-element.28.refs_4_.rest_4_), channel_id=1, source_target_pairs={{0,3},{1,0},{2,1},{3,2},{4,7},{5,4},{6,5},{7,6},{8,11},{9,8},{10,9... | collective-permute-start | bytes 1544 | tf_op jit(solution)/shard_map/ppermute | solution.py:526
  72.1 0.7 collective-permute-start.1
  72.8 3.3 %collective-permute-done.2.refs_6_.rest_6_ = f32[1,128]{1,0:T(1,128)S(1)} collective-permute-done((f32[1,128]{1,0:T(1,128)}, f32[1,128]{1,0:T(1,128)S(1)}, u32[]{:S(2)}, u32[]{:S(2)}) %collective-permute-start.2) | collective-permute-done | bytes 544 | tf_op jit(solution)/shard_map/ppermute | solution.py:526
  76.1 0.6 copy-done.14
  76.7 2.2 %all-to-all-done.1 = bf16[64,32,128]{2,1,0:T(8,128)(2,1)S(1)} async-done(((bf16[64,32,128]{2,1,0:T(8,128)(2,1)}), bf16[64,32,128]{2,1,0:T(8,128)(2,1)S(1)}, u32[]{:S(2)}, u32[]{:S(2)}) %all-to-all-start.1) | async-done | bytes 524320 | tf_op jit(solution)/shard_map/all_to_all | solution.py:520
  78.9 1.2 copy-done.2
  80.2 0.7 copy-done.11
  80.8 0.7 copy-done.15
  81.5 1.7 mr_project.1
  83.2 2.8 %collective-permute-start.6 = (f32[1,128]{1,0:T(1,128)S(1)}, f32[1,128]{1,0:T(1,128)S(1)}, u32[]{:S(2)}, u32[]{:S(2)}) collective-permute-start(f32[1,128]{1,0:T(1,128)S(1)} %get-tuple-element.29.rest_0_), channel_id=1, source_target_pairs={{0,3},{1,0},{2,1},{3,2},{4,7},{5,4},{6,5},{7,6},{8,11},{9,8},{10,9... | collective-permute-start | bytes 1544 | tf_op jit(solution)/shard_map/ppermute | solution.py:526
  86.3 0.7 collective-permute-start.4
  87.0 2.8 %collective-permute-done.5.rest_2_ = f32[1,128]{1,0:T(1,128)S(1)} collective-permute-done((f32[1,128]{1,0:T(1,128)S(1)}, f32[1,128]{1,0:T(1,128)S(1)}, u32[]{:S(2)}, u32[]{:S(2)}) %collective-permute-start.5) | collective-permute-done | bytes 544 | tf_op jit(solution)/shard_map/ppermute | solution.py:526
  90.5 4.5 %taps_grad_of.1 = (bf16[64,64,128]{2,1,0:T(8,128)(2,1)}, f32[2048,256]{1,0:T(8,128)}) custom-call(bf16[2048,128]{1,0:T(8,128)(2,1)} %bitcast.6, bf16[2048,128]{1,0:T(8,128)(2,1)} %key_li.3, bf16[2048,128]{1,0:T(8,128)(2,1)} %get-tuple-element.25.refs_2_.mixed, bf16[2048,128]{1,0:T(8,128)(2,1)} %query.3, f32[16,128]{1,0:T(8,128)} %bitcast.9, ...), custom_call_target="tpu_custom_call" | custom-call | tf_op jit(solution)/shard_map/taps_grad_of/pallas_call | solution.py:220
  95.0 9.6 %all-to-all-start.2 = ((bf16[64,64,128]{2,1,0:T(8,128)(2,1)}), bf16[64,64,128]{2,1,0:T(8,128)(2,1)S(1)}, u32[]{:S(2)}, u32[]{:S(2)}) async-start(bf16[64,64,128]{2,1,0:T(8,128)(2,1)} %get-tuple-element.36), calls=%async_computation.2 | async-start | bytes 2097152 | tf_op jit(solution)/shard_map/all_to_all | solution.py:520
  104.6 4.5 %product_grad_of.1 = (bf16[2048,128]{1,0:T(8,128)(2,1)}, bf16[2048,128]{1,0:T(8,128)(2,1)}, f32[2048,128]{1,0:T(8,128)}) custom-call(bf16[2048,128]{1,0:T(8,128)(2,1)} %bitcast.7, bf16[2048,128]{1,0:T(8,128)(2,1)} %key_li.3, bf16[2048,128]{1,0:T(8,128)(2,1)} %get-tuple-element.25.refs_2_.mixed, f32[2048,128]{1,0:T(8,128)} %get-tuple-element.26.conv, ...), custom_call_target="tpu_custom_call" | custom-call | tf_op jit(solution)/shard_map/product_grad_of/pallas_call | solution.py:220
  109.2 2.4 %collective-permute-start.7 = (bf16[2048,128]{1,0:T(8,128)(2,1)}, bf16[2048,128]{1,0:T(8,128)(2,1)S(1)}, u32[]{:S(2)}, u32[]{:S(2)}) collective-permute-start(bf16[2048,128]{1,0:T(8,128)(2,1)} %get-tuple-element.34), channel_id=1, source_target_pairs={{4,0},{8,4},{12,8},{16,12},{20,16},{24,20},{28,24},{32,28},{36,32}... | collective-permute-start | bytes 1572872 | tf_op jit(solution)/shard_map/ppermute | solution.py:532
  111.5 23.4 %collective-permute-done.7 = bf16[2048,128]{1,0:T(8,128)(2,1)S(1)} collective-permute-done((bf16[2048,128]{1,0:T(8,128)(2,1)}, bf16[2048,128]{1,0:T(8,128)(2,1)S(1)}, u32[]{:S(2)}, u32[]{:S(2)}) %collective-permute-start.7) | collective-permute-done | bytes 524320 | tf_op jit(solution)/shard_map/ppermute | solution.py:532
  134.9 0.8 copy-done.20
  135.7 4.9 %filter_grad.1 = bf16[64,72,128]{2,1,0:T(8,128)(2,1)} custom-call(bf16[64,64,128]{2,1,0:T(8,128)(2,1)S(1)} %all-to-all-done.2.refs_0_, f32[2048,256]{1,0:T(8,128)S(1)} %get-tuple-element.37.refs_1_, bf16[64,32,128]{2,1,0:T(8,128)(2,1)} %bitcast.1.refs_2_, bf16[128,128]{1,0:T(8,128)(2,1)S(1)} %copy-done.8, f32[64,128]{1,0:T(8,128)S(1)} %copy-done.10, ...), custom_call_target="tpu_custom_call" | custom-call | tf_op jit(solution)/shard_map/filter_grad/pallas_call | solution.py:264
  140.6 9.1 %all-to-all-start.3 = ((bf16[64,72,128]{2,1,0:T(8,128)(2,1)}), bf16[64,72,128]{2,1,0:T(8,128)(2,1)S(1)}, u32[]{:S(2)}, u32[]{:S(2)}) async-start(bf16[64,72,128]{2,1,0:T(8,128)(2,1)} %filter_grad.1), calls=%async_computation.3 | async-start | bytes 2359296 | tf_op jit(solution)/shard_map/all_to_all | solution.py:520
  149.8 2.3 %multiply_convert_fusion = (bf16[2048,128]{1,0:T(8,128)(2,1)}, bf16[2048,128]{1,0:T(8,128)(2,1)}) fusion(bf16[2048,128]{1,0:T(8,128)(2,1)S(1)} %copy-done.17, f32[2048,128]{1,0:T(8,128)S(1)} %copy-done.19, bf16[2048,128]{1,0:T(8,128)(2,1)} %copy-done.20, bf16[2048,128]{1,0:T(8,128)(2,1)S(1)} %copy-done.18), kind=kLoop, calls=%fused_computation | loop fusion | flops 2097152 | bytes 3670016 | tf_op jit(solution)/shard_map/convert_element_type | solution.py:562
  152.1 29.0 %all-to-all-done.3.refs_0_ = bf16[64,72,128]{2,1,0:T(8,128)(2,1)S(1)} async-done(((bf16[64,72,128]{2,1,0:T(8,128)(2,1)}), bf16[64,72,128]{2,1,0:T(8,128)(2,1)S(1)}, u32[]{:S(2)}, u32[]{:S(2)}) %all-to-all-start.3) | async-done | bytes 1179680 | tf_op jit(solution)/shard_map/all_to_all | solution.py:520
  181.2 1.4 deliver.1
  (54 shorter events, 1.6 us)
Async XLA Ops:
  2.8 42.5 %copy-start.3 = (bf16[256,256]{1,0:T(8,128)(2,1)S(1)}, bf16[256,256]{1,0:T(8,128)(2,1)}, u32[]{:S(2)}) copy-start(bf16[256,256]{1,0:T(8,128)(2,1)} %constant.35.clone.refs_5_.refs_7_) | copy-start | bytes 393220
  2.9 42.5 %copy-start.4 = (bf16[256,256]{1,0:T(8,128)(2,1)S(1)}, bf16[256,256]{1,0:T(8,128)(2,1)}, u32[]{:S(2)}) copy-start(bf16[256,256]{1,0:T(8,128)(2,1)} %constant.34.clone.refs_4_.refs_6_) | copy-start | bytes 393220
  2.9 42.5 %copy-start.7 = (bf16[64,256]{1,0:T(8,128)(2,1)S(1)}, bf16[64,256]{1,0:T(8,128)(2,1)}, u32[]{:S(2)}) copy-start(bf16[64,256]{1,0:T(8,128)(2,1)} %constant.37.refs_6_.refs_8_) | copy-start | bytes 98308
  2.9 42.5 %copy-start.8 = (bf16[128,128]{1,0:T(8,128)(2,1)S(1)}, bf16[128,128]{1,0:T(8,128)(2,1)}, u32[]{:S(2)}) copy-start(bf16[128,128]{1,0:T(8,128)(2,1)} %constant.36.refs_1_.refs_3_) | copy-start | bytes 98308
  2.9 42.5 %copy-start.9 = (f32[64,128]{1,0:T(8,128)S(1)}, f32[64,128]{1,0:T(8,128)}, u32[]{:S(2)}) copy-start(f32[64,128]{1,0:T(8,128)} %constant.33.clone.refs_3_.refs_5_) | copy-start | bytes 98308
  2.9 42.5 %copy-start.10 = (f32[64,128]{1,0:T(8,128)S(1)}, f32[64,128]{1,0:T(8,128)}, u32[]{:S(2)}) copy-start(f32[64,128]{1,0:T(8,128)} %constant.32.clone.refs_2_.refs_4_) | copy-start | bytes 98308
  2.9 41.9 %all-to-all-start = ((bf16[64,64,128]{2,1,0:T(8,128)(2,1)}), bf16[64,64,128]{2,1,0:T(8,128)(2,1)S(1)}, u32[]{:S(2)}, u32[]{:S(2)}) async-start(bf16[64,64,128]{2,1,0:T(8,128)(2,1)} %pair_up.1), calls=%async_computation | async-start | bytes 2097152 | tf_op jit(solution)/shard_map/all_to_all | solution.py:520
  18.0 26.6 %collective-permute-start = (bf16[2048,128]{1,0:T(8,128)(2,1)}, bf16[2048,128]{1,0:T(8,128)(2,1)S(1)}, u32[]{:S(2)}, u32[]{:S(2)}) collective-permute-start(bf16[2048,128]{1,0:T(8,128)(2,1)} %product_of.1), channel_id=1, source_target_pairs={{0,4},{4,8},{8,12},{12,16},{16,20},{20,24},{24,28},{28,32},{32,36}... | collective-permute-start | bytes 1572872 | tf_op jit(solution)/shard_map/ppermute | solution.py:532
  44.6 0.8 copy-start.21
  50.3 28.6 %all-to-all-start.1 = ((bf16[64,32,128]{2,1,0:T(8,128)(2,1)}), bf16[64,32,128]{2,1,0:T(8,128)(2,1)S(1)}, u32[]{:S(2)}, u32[]{:S(2)}) async-start(bf16[64,32,128]{2,1,0:T(8,128)(2,1)} %bitcast.1.refs_2_), calls=%async_computation.1 | async-start | bytes 1048576 | tf_op jit(solution)/shard_map/all_to_all | solution.py:520
  61.6 17.3 %copy-start.1 = (bf16[2048,128]{1,0:T(8,128)(2,1)S(1)}, bf16[2048,128]{1,0:T(8,128)(2,1)}, u32[]{:S(2)}) copy-start(bf16[2048,128]{1,0:T(8,128)(2,1)} %key_li.3) | copy-start | bytes 1572868
  61.6 17.3 %copy-start.5 = (f32[2048]{0:T(1024)S(1)}, f32[2048]{0:T(1024)}, u32[]{:S(2)}) copy-start(f32[2048]{0:T(1024)} %param.25) | copy-start | bytes 24580
  69.0 3.9 %collective-permute-start.3 = (f32[1,128]{1,0:T(1,128)}, f32[1,128]{1,0:T(1,128)S(1)}, u32[]{:S(2)}, u32[]{:S(2)}) collective-permute-start(f32[1,128]{1,0:T(1,128)} %get-tuple-element.28.refs_4_.rest_4_), channel_id=1, source_target_pairs={{0,3},{1,0},{2,1},{3,2},{4,7},{5,4},{6,5},{7,6},{8,11},{9,8},{10,9... | collective-permute-start | bytes 1544 | tf_op jit(solution)/shard_map/ppermute | solution.py:526
  71.8 4.3 %collective-permute-start.2 = (f32[1,128]{1,0:T(1,128)}, f32[1,128]{1,0:T(1,128)S(1)}, u32[]{:S(2)}, u32[]{:S(2)}) collective-permute-start(f32[1,128]{1,0:T(1,128)} %get-tuple-element.28.refs_4_.rest_4_), channel_id=1, source_target_pairs={{0,2},{1,3},{2,0},{3,1},{4,6},{5,7},{6,4},{7,5},{8,10},{9,11},{10,... | collective-permute-start | bytes 1544 | tf_op jit(solution)/shard_map/ppermute | solution.py:526
  72.1 4.0 %collective-permute-start.1 = (f32[1,128]{1,0:T(1,128)}, f32[1,128]{1,0:T(1,128)S(1)}, u32[]{:S(2)}, u32[]{:S(2)}) collective-permute-start(f32[1,128]{1,0:T(1,128)} %get-tuple-element.28.refs_4_.rest_4_), channel_id=1, source_target_pairs={{0,1},{1,2},{2,3},{3,0},{4,5},{5,6},{6,7},{7,4},{8,9},{9,10},{10,1... | collective-permute-start | bytes 1544 | tf_op jit(solution)/shard_map/ppermute | solution.py:526
  72.8 17.1 %copy-start.12 = (f32[1,128]{1,0:T(1,128)}, f32[1,128]{1,0:T(1,128)S(1)}, u32[]{:S(2)}) copy-start(f32[1,128]{1,0:T(1,128)S(1)} %collective-permute-done.3.refs_7_.rest_7_) | copy-start | bytes 1540
  76.1 13.9 %copy-start.13 = (f32[1,128]{1,0:T(1,128)}, f32[1,128]{1,0:T(1,128)S(1)}, u32[]{:S(2)}) copy-start(f32[1,128]{1,0:T(1,128)S(1)} %collective-permute-done.2.refs_6_.rest_6_) | copy-start | bytes 1540
  78.9 11.0 %copy-start = (bf16[64,32,128]{2,1,0:T(8,128)(2,1)}, bf16[64,32,128]{2,1,0:T(8,128)(2,1)S(1)}, u32[]{:S(2)}) copy-start(bf16[64,32,128]{2,1,0:T(8,128)(2,1)S(1)} %all-to-all-done.1) | copy-start | bytes 1572868
  78.9 1.2 copy-start.2
  83.2 6.8 %copy-start.16 = (f32[1,128]{1,0:T(1,128)}, f32[1,128]{1,0:T(1,128)S(1)}, u32[]{:S(2)}) copy-start(f32[1,128]{1,0:T(1,128)S(1)} %get-tuple-element.29.rest_0_) | copy-start | bytes 1540
  83.2 3.9 %collective-permute-start.6 = (f32[1,128]{1,0:T(1,128)S(1)}, f32[1,128]{1,0:T(1,128)S(1)}, u32[]{:S(2)}, u32[]{:S(2)}) collective-permute-start(f32[1,128]{1,0:T(1,128)S(1)} %get-tuple-element.29.rest_0_), channel_id=1, source_target_pairs={{0,3},{1,0},{2,1},{3,2},{4,7},{5,4},{6,5},{7,6},{8,11},{9,8},{10,9... | collective-permute-start | bytes 1544 | tf_op jit(solution)/shard_map/ppermute | solution.py:526
  86.0 3.9 %collective-permute-start.5 = (f32[1,128]{1,0:T(1,128)S(1)}, f32[1,128]{1,0:T(1,128)S(1)}, u32[]{:S(2)}, u32[]{:S(2)}) collective-permute-start(f32[1,128]{1,0:T(1,128)S(1)} %get-tuple-element.29.rest_0_), channel_id=1, source_target_pairs={{0,2},{1,3},{2,0},{3,1},{4,6},{5,7},{6,4},{7,5},{8,10},{9,11},{10,... | collective-permute-start | bytes 1544 | tf_op jit(solution)/shard_map/ppermute | solution.py:526
  86.3 3.6 %collective-permute-start.4 = (f32[1,128]{1,0:T(1,128)S(1)}, f32[1,128]{1,0:T(1,128)S(1)}, u32[]{:S(2)}, u32[]{:S(2)}) collective-permute-start(f32[1,128]{1,0:T(1,128)S(1)} %get-tuple-element.29.rest_0_), channel_id=1, source_target_pairs={{0,1},{1,2},{2,3},{3,0},{4,5},{5,6},{6,7},{7,4},{8,9},{9,10},{10,1... | collective-permute-start | bytes 1544 | tf_op jit(solution)/shard_map/ppermute | solution.py:526
  87.0 2.9 %copy-start.22 = (f32[1,128]{1,0:T(1,128)}, f32[1,128]{1,0:T(1,128)S(1)}, u32[]{:S(2)}) copy-start(f32[1,128]{1,0:T(1,128)S(1)} %collective-permute-done.6.rest_3_) | copy-start | bytes 1540
  95.0 40.7 %all-to-all-start.2 = ((bf16[64,64,128]{2,1,0:T(8,128)(2,1)}), bf16[64,64,128]{2,1,0:T(8,128)(2,1)S(1)}, u32[]{:S(2)}, u32[]{:S(2)}) async-start(bf16[64,64,128]{2,1,0:T(8,128)(2,1)} %get-tuple-element.36), calls=%async_computation.2 | async-start | bytes 2097152 | tf_op jit(solution)/shard_map/all_to_all | solution.py:520
  109.2 25.7 %collective-permute-start.7 = (bf16[2048,128]{1,0:T(8,128)(2,1)}, bf16[2048,128]{1,0:T(8,128)(2,1)S(1)}, u32[]{:S(2)}, u32[]{:S(2)}) collective-permute-start(bf16[2048,128]{1,0:T(8,128)(2,1)} %get-tuple-element.34), channel_id=1, source_target_pairs={{4,0},{8,4},{12,8},{16,12},{20,16},{24,20},{28,24},{32,28},{36,32}... | collective-permute-start | bytes 1572872 | tf_op jit(solution)/shard_map/ppermute | solution.py:532
  134.9 0.8 copy-start.20
  140.6 9.2 %copy-start.17 = (bf16[2048,128]{1,0:T(8,128)(2,1)S(1)}, bf16[2048,128]{1,0:T(8,128)(2,1)}, u32[]{:S(2)}) copy-start(bf16[2048,128]{1,0:T(8,128)(2,1)} %key.3) | copy-start | bytes 1572868
  140.6 9.2 %copy-start.18 = (bf16[2048,128]{1,0:T(8,128)(2,1)S(1)}, bf16[2048,128]{1,0:T(8,128)(2,1)}, u32[]{:S(2)}) copy-start(bf16[2048,128]{1,0:T(8,128)(2,1)} %value.3) | copy-start | bytes 1572868
  140.6 9.2 %copy-start.19 = (f32[2048,128]{1,0:T(8,128)S(1)}, f32[2048,128]{1,0:T(8,128)}, u32[]{:S(2)}) copy-start(f32[2048,128]{1,0:T(8,128)} %get-tuple-element.33) | copy-start | bytes 3145732
  140.6 40.5 %all-to-all-start.3 = ((bf16[64,72,128]{2,1,0:T(8,128)(2,1)}), bf16[64,72,128]{2,1,0:T(8,128)(2,1)S(1)}, u32[]{:S(2)}, u32[]{:S(2)}) async-start(bf16[64,72,128]{2,1,0:T(8,128)(2,1)} %filter_grad.1), calls=%async_computation.3 | async-start | bytes 2359296 | tf_op jit(solution)/shard_map/all_to_all | solution.py:520
  149.8 31.4 %copy-start.6 = (f32[2048]{0:T(1024)S(1)}, f32[2048]{0:T(1024)}, u32[]{:S(2)}) copy-start(f32[2048]{0:T(1024)} %param.25) | copy-start | bytes 24580
  (5 other events, 2.9 us)
